TPU v7x, 128 devices: a whole 4x4x4 slice. The times are simulated.
128 devices in a mesh: fsdp: 8 (over y, x_lo), ctx: 4 (over x_hi, core), tp: 4 (over z).
Axes of the slice: x: 4 (x_hi: 2, x_lo: 2; x = x_hi * 2 + x_lo), y: 4, z: 4, core: 2. Of those that a mesh axis runs over, the one named last changes fastest.
Arguments:
- block_input: bfloat16 [8192, 1024], P(('fsdp', 'ctx')), may hold values from -6 to 6
- cotangent: bfloat16 [8192, 1024], P(('fsdp', 'ctx')), may hold values from -6 to 6
- sequence_starts: int32 [8, 2], P('fsdp'), may hold values from 1 to 1023, as said below
- attention_weight: float32 [2, 1024, 4, 1024], P(None, ('fsdp', 'ctx'), None, 'tp')
- attention_first: float32 [2, 1024, 4, 1024], P(None, ('fsdp', 'ctx'), None, 'tp'), may hold values from -32 to 32
- attention_second: float32 [2, 1024, 4, 1024], P(None, ('fsdp', 'ctx'), None, 'tp'), may hold values from 106.496 to 425.984
- feedforward_weight: float32 [2, 1024, 2, 4096], P(None, ('fsdp', 'ctx'), None, 'tp'), may hold values from -0.1875 to 0.1875
- feedforward_first: float32 [2, 1024, 2, 4096], P(None, ('fsdp', 'ctx'), None, 'tp'), may hold values from -32 to 32
- feedforward_second: float32 [2, 1024, 2, 4096], P(None, ('fsdp', 'ctx'), None, 'tp'), may hold values from 147.456 to 589.824
- vector_weight: float32 [2, 12, 1024], P(None, None, ('fsdp', 'ctx', 'tp'))
- vector_first: float32 [2, 12, 1024], P(None, None, ('fsdp', 'ctx', 'tp')), may hold values from -64 to 64
- vector_second: float32 [2, 12, 1024], P(None, None, ('fsdp', 'ctx', 'tp')), may hold values from 409.6 to 1638.4
Outputs:
- block_output: float32 [8192, 1024], P(('fsdp', 'ctx'))
- input_gradient: float32 [8192, 1024], P(('fsdp', 'ctx'))
- attention_moment: float32 [2, 1024, 4, 1024], P(None, ('fsdp', 'ctx'), None, 'tp')
- attention_square: float32 [2, 1024, 4, 1024], P(None, ('fsdp', 'ctx'), None, 'tp')
- attention_updated: float32 [2, 1024, 4, 1024], P(None, ('fsdp', 'ctx'), None, 'tp')
- feedforward_moment: float32 [2, 1024, 2, 4096], P(None, ('fsdp', 'ctx'), None, 'tp')
- feedforward_square: float32 [2, 1024, 2, 4096], P(None, ('fsdp', 'ctx'), None, 'tp')
- feedforward_updated: float32 [2, 1024, 2, 4096], P(None, ('fsdp', 'ctx'), None, 'tp')
- vector_moment: float32 [2, 12, 1024], P(None, None, ('fsdp', 'ctx', 'tp'))
- vector_square: float32 [2, 12, 1024], P(None, None, ('fsdp', 'ctx', 'tp'))
- vector_updated: float32 [2, 12, 1024], P(None, None, ('fsdp', 'ctx', 'tp'))
Inputs may be any that keep to these rules, and one draw needn't show every extreme that they name: `sequence_starts`: A group's sequences run from 0 to its first start, between the starts, and from the second start to 1024; the first start is below 256, the second above 768.
All inputs are finite; a program needn't handle non-finite values.
Results may differ from a plain program's by a relative error of at most 0.04.
Values may be sent and summed in bfloat16 or wider, within the bound.
No kernel may reach another device: no remote copies, remote signals or barrier semaphores. Data moves between devices by JAX's collectives and lax.ppermute only.
A program may use at most 128 MiB of HBM per device.

v0:
```python
import jax
import jax.numpy as jnp
from jax import lax
from jax.sharding import PartitionSpec as P

H = 16
HD = 64
STEP = 10


norm_eps = 1e-05
gelu_factor = 0.7978845608028654
matrix_rate = 0.05
vector_rate = 0.3
weight_decay = 0.1


def layer_norm(values, gain_row, shift_row):
    centre = values - jnp.mean(values, axis=-1, keepdims=True)
    spread = jnp.mean(centre * centre, axis=-1, keepdims=True)
    return centre * lax.rsqrt(spread + norm_eps) * gain_row + shift_row


def gelu_tanh(values):
    return (
        0.5
        * values
        * (1.0 + jnp.tanh(gelu_factor * (values + 0.044715 * values * values * values)))
    )


def segment_of(position, bounds):
    return (position >= bounds[0]).astype(jnp.int32) + (position >= bounds[1]).astype(jnp.int32)


def adamw_step(weight, moment, second, gradient, step_rate, decay_rate):
    moment = 0.9 * moment + 0.1 * gradient
    second = 0.95 * second + 0.05 * gradient * gradient
    first_fix = 1.0 - 0.9**STEP
    second_fix = 1.0 - 0.95**STEP
    update = moment / first_fix / (jnp.sqrt(second / second_fix) + 1e-08) + decay_rate * weight
    return (moment, second, weight - step_rate * update)


def tensor_sum(partial_value):
    return lax.psum(partial_value.astype(jnp.bfloat16), "tp").astype(jnp.float32)


def contract_last(left_side, right_side):
    return lax.dot_general(
        left_side, right_side, (((1,), (1,)), ((), ())), preferred_element_type=jnp.float32
    )


def contract_first(left_side, right_side):
    return lax.dot_general(
        left_side, right_side, (((0,), (0,)), ((), ())), preferred_element_type=jnp.float32
    )


def block_scores(query_rows, key_heads, row_start, bounds, slopes):
    block_rows = query_rows.shape[0]
    length = key_heads.shape[0]
    key_place = jnp.arange(length, dtype=jnp.int32)
    row_place = row_start + jnp.arange(block_rows, dtype=jnp.int32)
    distance = (row_place[:, None] - key_place[None, :]).astype(jnp.float32)
    raw_scores = (
        jnp.einsum("qhe,khe->hqk", query_rows, key_heads, preferred_element_type=jnp.float32)
        * 0.125
        - slopes[:, None, None] * distance[None]
    )
    allowed = (segment_of(row_place, bounds)[:, None] == segment_of(key_place, bounds)[None, :]) & (
        row_place[:, None] >= key_place[None, :]
    )
    return jnp.where(allowed[None], raw_scores, -1e30)


def attend_forward(queries, key_rows, value_rows, bounds, slopes):
    length = queries.shape[0]
    head_count = slopes.shape[0]
    block_rows = min(512, length)
    query_heads = queries.reshape(length, head_count, HD)
    key_heads = key_rows.reshape(length, head_count, HD)
    value_heads = value_rows.reshape(length, head_count, HD)

    def one_block(row_start):
        query_rows = lax.dynamic_slice_in_dim(query_heads, row_start, block_rows, 0)
        scores = block_scores(query_rows, key_heads, row_start, bounds, slopes)
        top_score = jnp.max(scores, axis=-1, keepdims=True)
        exponent = jnp.exp(scores - top_score)
        totals = jnp.sum(exponent, axis=-1, keepdims=True)
        softmax_rows = (exponent / totals).astype(jnp.bfloat16)
        mixed_rows = jnp.einsum(
            "hqk,khe->qhe", softmax_rows, value_heads, preferred_element_type=jnp.float32
        )
        return (
            mixed_rows.astype(jnp.bfloat16).reshape(block_rows, head_count * HD),
            (top_score + jnp.log(totals))[:, :, 0],
        )

    starts = jnp.arange(length // block_rows, dtype=jnp.int32) * block_rows
    mixed_rows, log_totals = lax.map(one_block, starts)
    return (mixed_rows.reshape(length, head_count * HD), log_totals)


def attend_backward(queries, key_rows, value_rows, back_mixed, log_totals, bounds, slopes):
    length = queries.shape[0]
    head_count = slopes.shape[0]
    block_rows = min(512, length)
    query_heads = queries.reshape(length, head_count, HD)
    key_heads = key_rows.reshape(length, head_count, HD)
    value_heads = value_rows.reshape(length, head_count, HD)
    back_heads = back_mixed.reshape(length, head_count, HD)

    def one_block(running, inputs):
        back_keys, back_values = running
        row_start, log_rows = inputs
        query_rows = lax.dynamic_slice_in_dim(query_heads, row_start, block_rows, 0)
        back_rows = lax.dynamic_slice_in_dim(back_heads, row_start, block_rows, 0)
        scores = block_scores(query_rows, key_heads, row_start, bounds, slopes)
        softmax_rows = jnp.exp(scores - log_rows[:, :, None])
        back_prob = jnp.einsum(
            "qhe,khe->hqk", back_rows, value_heads, preferred_element_type=jnp.float32
        )
        row_delta = jnp.sum(softmax_rows * back_prob, axis=-1, keepdims=True)
        back_scores = (softmax_rows * (back_prob - row_delta)).astype(jnp.bfloat16)
        back_query = (
            jnp.einsum("hqk,khe->qhe", back_scores, key_heads, preferred_element_type=jnp.float32)
            * 0.125
        )
        back_keys = (
            back_keys
            + jnp.einsum(
                "hqk,qhe->khe", back_scores, query_rows, preferred_element_type=jnp.float32
            )
            * 0.125
        )
        back_values = back_values + jnp.einsum(
            "hqk,qhe->khe",
            softmax_rows.astype(jnp.bfloat16),
            back_rows,
            preferred_element_type=jnp.float32,
        )
        return ((back_keys, back_values), back_query.astype(jnp.bfloat16))

    starts = jnp.arange(length // block_rows, dtype=jnp.int32) * block_rows
    zero_heads = jnp.zeros((length, head_count, HD), jnp.float32)
    (back_keys, back_values), back_query = lax.scan(
        one_block, (zero_heads, zero_heads), (starts, log_totals)
    )
    flat_width = head_count * HD
    return (
        back_query.reshape(length, flat_width),
        back_keys.astype(jnp.bfloat16).reshape(length, flat_width),
        back_values.astype(jnp.bfloat16).reshape(length, flat_width),
    )


def body(
    block_input,
    cotangent,
    sequence_starts,
    attention_weight,
    attention_first,
    attention_second,
    feedforward_weight,
    feedforward_first,
    feedforward_second,
    vector_weight,
    vector_first,
    vector_second,
):
    context_count = lax.axis_size("ctx")
    tensor_rank = lax.axis_index("tp")
    context_rank = lax.axis_index("ctx")
    model_width = block_input.shape[1]
    layer_count = attention_weight.shape[0]
    head_width = attention_weight.shape[3]
    hidden_width = feedforward_weight.shape[3]
    local_heads = head_width // context_count // HD
    first_head = tensor_rank * (head_width // HD) + context_rank * local_heads
    slopes = jnp.exp2(
        -8.0
        * ((first_head + jnp.arange(local_heads, dtype=jnp.int32)).astype(jnp.float32) + 1.0)
        / H
    )
    bounds = sequence_starts[0]
    owner_mask = (tensor_rank == 0).astype(jnp.float32)
    vectors = lax.all_gather(vector_weight, ("fsdp", "ctx", "tp"), axis=2, tiled=True)
    stream = block_input.astype(jnp.float32)
    saved_acts = []
    for layer_index in range(layer_count):
        attention_full = lax.all_gather(
            attention_weight[layer_index].astype(jnp.bfloat16), ("fsdp", "ctx"), axis=0, tiled=True
        )
        feedforward_full = lax.all_gather(
            feedforward_weight[layer_index].astype(jnp.bfloat16),
            ("fsdp", "ctx"),
            axis=0,
            tiled=True,
        )
        vector = vectors[layer_index]
        project_full = attention_full[:, :3].reshape(model_width, 3 * head_width)
        bias_query = lax.dynamic_slice_in_dim(vector[2], tensor_rank * head_width, head_width)
        bias_value = lax.dynamic_slice_in_dim(vector[3], tensor_rank * head_width, head_width)
        bias_hidden = lax.dynamic_slice_in_dim(
            vector[8:].reshape(-1), tensor_rank * hidden_width, hidden_width
        )
        normed = layer_norm(stream, vector[0], vector[1]).astype(jnp.bfloat16)
        project = jnp.dot(normed, project_full, preferred_element_type=jnp.float32)
        queries = (project[:, :head_width] + bias_query).astype(jnp.bfloat16)
        key_rows = project[:, head_width : 2 * head_width].astype(jnp.bfloat16)
        value_rows = (project[:, 2 * head_width :] + bias_value).astype(jnp.bfloat16)
        query_heads, key_heads, value_heads = (
            lax.all_to_all(queries, "ctx", split_axis=1, concat_axis=0, tiled=True),
            lax.all_to_all(key_rows, "ctx", split_axis=1, concat_axis=0, tiled=True),
            lax.all_to_all(value_rows, "ctx", split_axis=1, concat_axis=0, tiled=True),
        )
        mixed_heads, log_totals = attend_forward(
            query_heads, key_heads, value_heads, bounds, slopes
        )
        mixed_rows = lax.all_to_all(mixed_heads, "ctx", split_axis=0, concat_axis=1, tiled=True)
        middle = stream + tensor_sum(contract_last(mixed_rows, attention_full[:, 3])) + vector[4]
        normed_two = layer_norm(middle, vector[5], vector[6]).astype(jnp.bfloat16)
        hidden = (
            jnp.dot(normed_two, feedforward_full[:, 0], preferred_element_type=jnp.float32)
            + bias_hidden
        )
        active = gelu_tanh(hidden).astype(jnp.bfloat16)
        out_stream = middle + tensor_sum(contract_last(active, feedforward_full[:, 1])) + vector[7]
        kept_weights = None
        saved_acts.append(
            (
                stream,
                normed,
                query_heads,
                key_heads,
                value_heads,
                log_totals,
                mixed_rows,
                middle,
                normed_two,
                hidden,
                active,
                kept_weights,
            )
        )
        stream = out_stream
    back_stream = cotangent.astype(jnp.float32)
    attention_grads = [None] * layer_count
    feedforward_grads = [None] * layer_count
    vector_grads = [None] * layer_count
    for layer_index in reversed(range(layer_count)):
        (
            layer_in,
            normed,
            query_heads,
            key_heads,
            value_heads,
            log_totals,
            mixed_rows,
            middle,
            normed_two,
            hidden,
            active,
            kept_weights,
        ) = saved_acts[layer_index]
        attention_full, feedforward_full = (
            lax.all_gather(
                attention_weight[layer_index].astype(jnp.bfloat16),
                ("fsdp", "ctx"),
                axis=0,
                tiled=True,
            ),
            lax.all_gather(
                feedforward_weight[layer_index].astype(jnp.bfloat16),
                ("fsdp", "ctx"),
                axis=0,
                tiled=True,
            ),
        )
        vector = vectors[layer_index]
        back_branch = back_stream.astype(jnp.bfloat16)
        back_down = contract_first(back_branch, active)
        back_active = jnp.dot(
            back_branch, feedforward_full[:, 1], preferred_element_type=jnp.float32
        )
        back_hidden = jax.vjp(gelu_tanh, hidden)[1](back_active)[0].astype(jnp.bfloat16)
        back_up = contract_first(normed_two, back_hidden)
        back_normed_two = tensor_sum(contract_last(back_hidden, feedforward_full[:, 0]))
        norm_two_back = jax.vjp(layer_norm, middle, vector[5], vector[6])[1](back_normed_two)
        back_middle = back_stream + norm_two_back[0]
        back_attn = back_middle.astype(jnp.bfloat16)
        back_dense = contract_first(back_attn, mixed_rows)
        back_mixed = jnp.dot(
            back_attn, attention_full[:, 3], preferred_element_type=jnp.float32
        ).astype(jnp.bfloat16)
        back_heads = lax.all_to_all(back_mixed, "ctx", split_axis=1, concat_axis=0, tiled=True)
        head_query, head_keys, head_values = attend_backward(
            query_heads, key_heads, value_heads, back_heads, log_totals, bounds, slopes
        )
        back_query, back_keys, back_values = (
            lax.all_to_all(head_query, "ctx", split_axis=0, concat_axis=1, tiled=True),
            lax.all_to_all(head_keys, "ctx", split_axis=0, concat_axis=1, tiled=True),
            lax.all_to_all(head_values, "ctx", split_axis=0, concat_axis=1, tiled=True),
        )
        back_project = jnp.concatenate([back_query, back_keys, back_values], axis=1)
        back_qkv = contract_first(normed, back_project).reshape(model_width, 3, head_width)
        project_full = attention_full[:, :3].reshape(model_width, 3 * head_width)
        back_normed = tensor_sum(contract_last(back_project, project_full))
        norm_one_back = jax.vjp(layer_norm, layer_in, vector[0], vector[1])[1](back_normed)
        back_stream = back_middle + norm_one_back[0]
        attention_grads[layer_index] = jnp.concatenate([back_qkv, back_dense[:, None]], axis=1)
        feedforward_grads[layer_index] = jnp.stack([back_up, back_down], axis=1)
        zero_row = jnp.zeros((model_width,), jnp.float32)
        query_row = lax.dynamic_update_slice_in_dim(
            zero_row, jnp.sum(back_query, axis=0, dtype=jnp.float32), tensor_rank * head_width, 0
        )
        value_row = lax.dynamic_update_slice_in_dim(
            zero_row, jnp.sum(back_values, axis=0, dtype=jnp.float32), tensor_rank * head_width, 0
        )
        hidden_zero = jnp.zeros(((vector.shape[0] - 8) * model_width,), jnp.float32)
        hidden_rows = lax.dynamic_update_slice_in_dim(
            hidden_zero,
            jnp.sum(back_hidden, axis=0, dtype=jnp.float32),
            tensor_rank * hidden_width,
            0,
        ).reshape(-1, model_width)
        shared_rows = jnp.stack(
            [
                norm_one_back[1] * owner_mask,
                norm_one_back[2] * owner_mask,
                query_row,
                value_row,
                jnp.sum(back_attn, axis=0, dtype=jnp.float32) * owner_mask,
                norm_two_back[1] * owner_mask,
                norm_two_back[2] * owner_mask,
                jnp.sum(back_branch, axis=0, dtype=jnp.float32) * owner_mask,
            ]
        )
        vector_grads[layer_index] = jnp.concatenate([shared_rows, hidden_rows], axis=0)
        attention_owned, feedforward_owned = (
            lax.psum_scatter(
                attention_grads[layer_index].astype(jnp.bfloat16),
                ("fsdp", "ctx"),
                scatter_dimension=0,
                tiled=True,
            ).astype(jnp.float32),
            lax.psum_scatter(
                feedforward_grads[layer_index].astype(jnp.bfloat16),
                ("fsdp", "ctx"),
                scatter_dimension=0,
                tiled=True,
            ).astype(jnp.float32),
        )
        attention_grads[layer_index] = attention_owned
        feedforward_grads[layer_index] = feedforward_owned
    attention_total = jnp.stack(attention_grads)
    feedforward_total = jnp.stack(feedforward_grads)
    vector_total = lax.psum_scatter(
        jnp.stack(vector_grads), ("fsdp", "ctx", "tp"), scatter_dimension=2, tiled=True
    )
    attention_moment, attention_square, attention_updated = adamw_step(
        attention_weight,
        attention_first,
        attention_second,
        attention_total,
        matrix_rate,
        weight_decay,
    )
    feedforward_moment, feedforward_square, feedforward_updated = adamw_step(
        feedforward_weight,
        feedforward_first,
        feedforward_second,
        feedforward_total,
        matrix_rate,
        weight_decay,
    )
    vector_moment, vector_square, vector_updated = adamw_step(
        vector_weight, vector_first, vector_second, vector_total, vector_rate, 0.0
    )
    return (
        stream,
        back_stream,
        attention_moment,
        attention_square,
        attention_updated,
        feedforward_moment,
        feedforward_square,
        feedforward_updated,
        vector_moment,
        vector_square,
        vector_updated,
    )


def solution(mesh):
    in_specs = (
        P(("fsdp", "ctx"), None),
        P(("fsdp", "ctx"), None),
        P("fsdp", None),
        P(None, ("fsdp", "ctx"), None, "tp"),
        P(None, ("fsdp", "ctx"), None, "tp"),
        P(None, ("fsdp", "ctx"), None, "tp"),
        P(None, ("fsdp", "ctx"), None, "tp"),
        P(None, ("fsdp", "ctx"), None, "tp"),
        P(None, ("fsdp", "ctx"), None, "tp"),
        P(None, None, ("fsdp", "ctx", "tp")),
        P(None, None, ("fsdp", "ctx", "tp")),
        P(None, None, ("fsdp", "ctx", "tp")),
    )
    out_specs = (
        P(("fsdp", "ctx"), None),
        P(("fsdp", "ctx"), None),
        P(None, ("fsdp", "ctx"), None, "tp"),
        P(None, ("fsdp", "ctx"), None, "tp"),
        P(None, ("fsdp", "ctx"), None, "tp"),
        P(None, ("fsdp", "ctx"), None, "tp"),
        P(None, ("fsdp", "ctx"), None, "tp"),
        P(None, ("fsdp", "ctx"), None, "tp"),
        P(None, None, ("fsdp", "ctx", "tp")),
        P(None, None, ("fsdp", "ctx", "tp")),
        P(None, None, ("fsdp", "ctx", "tp")),
    )
    return jax.shard_map(body, mesh=mesh, in_specs=in_specs, out_specs=out_specs, check_vma=False)
```

profile of v0, /device:TPU:0, one launch (start us, length us, event | category | flops | bytes accessed | tf_op | source)
XLA Modules:
  0.0 1710.1 jit_solution(17888975004173497862)
XLA Ops:
  8.9 324.8 %all_gather.19 = f32[2,12,1024]{1,2,0:T(8,128)S(1)} all-gather(f32[2,12,8]{1,2,0:T(8,128)} %param.29), channel_id=1, replica_groups=mesh['fsdp'=8,'ctx'=4,'tp'=4] {'fsdp','ctx','tp'}, dimensions={2}, use_global_device_ids=true | all-gather | bytes 99072 | tf_op jit(solution)/shard_map/all_gather | solution.py:189
  333.7 4.7 fusion.167
  339.2 4.4 copy.204
  351.1 5.3 all-to-all-done
  360.6 5.3 all-to-all-done.1
  370.7 4.5 all-to-all-done.2
  376.7 23.3 %while.54 = (s32[]{:T(128)}, bf16[2,512,64]{1,2,0:T(8,128)(2,1)S(1)}, f32[2,1,512]{2,1,0:T(1,128)}, s32[2]{0:T(128)}, s32[2]{0:T(128)S(1)}, /*index=5*/bf16[1024...) while((s32[]{:T(128)}, ...), condition=%wide.region_5.6_spmd, body=%wide.region_2.5_spmd.sunk | while | flops 142122496 | bytes 6722267 | solution.py:102
  400.2 8.5 all_to_all.280
  413.3 34.7 %all-reduce.15.cloned.1.call-done = bf16[256,1024]{1,0:T(8,128)(2,1)} async-done(((bf16[256,1024]{1,0:T(8,128)(2,1)}), bf16[256,1024]{1,0:T(8,128)(2,1)}) %all-reduce.15.cloned.1.call-update) | async-done | bytes 524304 | tf_op jit(solution)/shard_map/psum | solution.py:46
  450.8 59.9 %all-gather.11.cloned.1.call-done = bf16[1,1024,2,1024]{3,1,2,0:T(8,128)(2,1)} async-done(((bf16[1,32,2,1024]{3,1,2,0:T(8,128)(2,1)}), bf16[1,1024,2,1024]{3,1,2,0:T(8,128)(2,1)}) %all-gather.11.cloned.1.call-update) | async-done | bytes 4194320 | tf_op jit(solution)/shard_map/all_gather | solution.py:196
  517.4 52.0 %all-gather.13.cloned.1.call-done = bf16[1,1024,4,256]{3,2,0,1:T(4,128)(2,1)} async-done(((bf16[1,32,4,256]{3,2,0,1:T(4,128)(2,1)}), bf16[1,1024,4,256]{3,2,0,1:T(4,128)(2,1)}) %all-gather.13.cloned.1.call-update) | async-done | bytes 2097168 | tf_op jit(solution)/shard_map/all_gather | solution.py:193
  569.4 4.4 copy.216
  576.5 38.3 %all-reduce.17.cloned.1.call-done = bf16[256,1024]{1,0:T(8,128)(2,1)} async-done(((bf16[256,1024]{1,0:T(8,128)(2,1)}), bf16[256,1024]{1,0:T(8,128)(2,1)}) %all-reduce.17.cloned.1.call-update) | async-done | bytes 524304 | tf_op jit(solution)/shard_map/psum | solution.py:46
  618.2 4.2 all-to-all-start.4
  623.3 5.4 all-to-all-done.4
  628.6 3.3 all-to-all-start.5
  632.7 5.3 all-to-all-done.5
  643.1 4.4 all-to-all-done.6
  648.9 23.4 %while.55 = (s32[]{:T(128)}, bf16[2,512,64]{1,2,0:T(8,128)(2,1)S(1)}, f32[2,1,512]{2,1,0:T(1,128)}, s32[2]{0:T(128)}, s32[2]{0:T(128)S(1)}, /*index=5*/bf16[1024...) while((s32[]{:T(128)}, ...), condition=%wide.region_15.16_spmd, body=%wide.region_12.15_spmd.sunk | while | flops 142122496 | bytes 6722267 | solution.py:102
  672.6 8.5 all_to_all.281
  684.7 40.0 %all-reduce.19.cloned.1.call-done = bf16[256,1024]{1,0:T(8,128)(2,1)} async-done(((bf16[256,1024]{1,0:T(8,128)(2,1)}), bf16[256,1024]{1,0:T(8,128)(2,1)}) %all-reduce.19.cloned.1.call-update) | async-done | bytes 524304 | tf_op jit(solution)/shard_map/psum | solution.py:46
  726.3 61.1 %all-gather.15.cloned.1.call-done = bf16[1,1024,2,1024]{3,1,2,0:T(8,128)(2,1)} async-done(((bf16[1,32,2,1024]{3,1,2,0:T(8,128)(2,1)}), bf16[1,1024,2,1024]{3,1,2,0:T(8,128)(2,1)}) %all-gather.15.cloned.1.call-update) | async-done | bytes 4194320 | tf_op jit(solution)/shard_map/all_gather | solution.py:196
  794.8 42.8 %all-reduce.21.cloned.1.call-done = bf16[256,1024]{1,0:T(8,128)(2,1)} async-done(((bf16[256,1024]{1,0:T(8,128)(2,1)}), bf16[256,1024]{1,0:T(8,128)(2,1)}) %all-reduce.21.cloned.1.call-update) | async-done | bytes 524304 | tf_op jit(solution)/shard_map/psum | solution.py:46
  845.8 4.2 all-to-all-start.8
  850.0 6.1 all-to-all-done.8
  857.6 34.2 %while.56 = (s32[]{:T(128)}, f32[1024,1,64]{0,2,1:T(8,128)}, f32[1024,1,64]{0,2,1:T(8,128)S(1)}, bf16[2,512,1,64]{1,3,2,0:T(8,128)(2,1)}, s32[2]{0:T(128)}, /*in...) while((s32[]{:T(128)}, f32[1024,1,64]{0,2,1:T(8,128)}, ...), condition=%wide.region_25.26_spmd.clone, body=%wide.region_23.25_spmd.clone.sunk | while | flops 344333824 | bytes 18574144 | solution.py:148
  897.7 4.4 all-to-all-done.11
  905.4 3.7 fusion.80
  911.5 4.1 all-to-all-start.9
  916.2 5.5 all-to-all-done.9
  928.2 36.5 %all-reduce.23.cloned.1.call-done = bf16[256,1024]{1,0:T(8,128)(2,1)} async-done(((bf16[256,1024]{1,0:T(8,128)(2,1)}), bf16[256,1024]{1,0:T(8,128)(2,1)}) %all-reduce.23.cloned.1.call-update) | async-done | bytes 524304 | tf_op jit(solution)/shard_map/psum | solution.py:46
  975.0 4.2 copy.239
  980.7 4.5 pad_maximum_fusion.3
  985.2 33.5 %all-reduce.25.cloned.1.call-done = bf16[256,1024]{1,0:T(8,128)(2,1)} async-done(((bf16[256,1024]{1,0:T(8,128)(2,1)}), bf16[256,1024]{1,0:T(8,128)(2,1)}) %all-reduce.25.cloned.1.call-update) | async-done | bytes 524304 | tf_op jit(solution)/shard_map/psum | solution.py:46
  1027.3 4.2 all-to-all-start.12
  1032.1 5.5 all-to-all-done.12
  1039.2 32.9 %while.57 = (s32[]{:T(128)}, f32[1024,1,64]{0,2,1:T(8,128)}, f32[1024,1,64]{0,2,1:T(8,128)S(1)}, bf16[2,512,1,64]{1,3,2,0:T(8,128)(2,1)}, s32[2]{0:T(128)}, /*in...) while((s32[]{:T(128)}, f32[1024,1,64]{0,2,1:T(8,128)}, ...), condition=%wide.region_34.35_spmd.clone, body=%wide.region_32.34_spmd.clone.sunk | while | flops 344333824 | bytes 18574144 | solution.py:148
  1072.9 3.5 all-to-all-start.15
  1078.9 3.7 all-to-all-done.15
  1088.0 4.0 all-to-all-done.14
  1095.4 6.0 all-to-all-done.13
  1110.5 36.8 %all-reduce.31.cloned.1.call-done = (bf16[256,1024]{1,0:T(8,128)(2,1)}, bf16[256,1024]{1,0:T(8,128)(2,1)}) async-done(((bf16[256,1024]{1,0:T(8,128)(2,1)}, bf16[256,1024]{1,0:T(8,128)(2,1)}), (bf16[256,1024]{1,0:T(8,128)(2,1)}, bf16[256,1024]{1,0:T(8,128)(2,1)})) %all-reduce.31.cloned.1.call-update) | async-done | bytes 1048592 | tf_op jit(solution)/shard_map/psum | solution.py:46
  1151.8 4.2 pad_maximum_fusion.2
  1170.2 3.5 add_add_fusion.4
  1173.8 126.4 %all-reduce.27.cloned.1.call-done = f32[2,12,1024]{1,0,2:T(2,128)} async-done(((f32[2,12,1024]{1,0,2:T(2,128)}), f32[2,12,1024]{1,0,2:T(2,128)}) %all-reduce.27.cloned.1.call-update) | async-done | bytes 98320
  1301.5 112.9 %all-reduce.29.cloned.1.call-done = (bf16[1024,4,256]{2,1,0:T(4,128)(2,1)}, bf16[1024,4,256]{2,1,0:T(4,128)(2,1)}) async-done(((bf16[1024,4,256]{2,1,0:T(4,128)(2,1)}, bf16[1024,4,256]{2,1,0:T(4,128)(2,1)}), (bf16[1024,4,256]{2,1,0:T(4,128)(2,1)}, bf16[1024,4,256]{2,1,0:T(4,128)(2,1)})) %all-reduce.29.cloned.1.call-update) | async-done | bytes 4194320
  1417.6 139.1 %reduce-scatter.5.cloned.1.call-done = bf16[32,2,1024]{2,0,1:T(8,128)(2,1)} async-done(((bf16[1024,2,1024]{2,0,1:T(8,128)(2,1)}), bf16[32,2,1024]{2,0,1:T(8,128)(2,1)}) %reduce-scatter.5.cloned.1.call-update) | async-done | bytes 131088 | tf_op jit(solution)/shard_map/reduce_scatter | solution.py:349
  1556.7 141.1 %reduce-scatter.3.cloned.1.call-done = bf16[32,2,1024]{2,0,1:T(8,128)(2,1)} async-done(((bf16[1024,2,1024]{2,0,1:T(8,128)(2,1)}), bf16[32,2,1024]{2,0,1:T(8,128)(2,1)}) %reduce-scatter.3.cloned.1.call-update) | async-done | bytes 131088 | tf_op jit(solution)/shard_map/reduce_scatter | solution.py:349
  (573 shorter events, 257.6 us)
Async XLA Ops:
  7.2 332.0 %all-gather.9.cloned.1.call-start = ((), (), s32[]{:S(2)}) async-start(), calls=%async_computation.26 | async-start | bytes 2162688 | tf_op jit(solution)/shard_map/all_gather | solution.py:193
  347.0 9.4 all-to-all-start
  356.4 9.4 all-to-all-start.1
  365.8 9.4 all-to-all-start.2
  369.2 78.8 %all-reduce.15.cloned.1.call-start = ((), (), s32[]{:S(2)}) async-start(), calls=%async_computation.18 | async-start | bytes 1048576 | tf_op jit(solution)/shard_map/psum | solution.py:46
  411.0 99.7 %all-gather.11.cloned.1.call-start = ((), (), s32[]{:S(2)}) async-start(), calls=%async_computation.27 | async-start | bytes 4325376 | tf_op jit(solution)/shard_map/all_gather | solution.py:196
  411.9 157.5 %all-gather.13.cloned.1.call-start = ((), (), s32[]{:S(2)}) async-start(), calls=%async_computation.28 | async-start | bytes 2162688 | tf_op jit(solution)/shard_map/all_gather | solution.py:193
  412.5 202.3 %all-reduce.17.cloned.1.call-start = ((), (), s32[]{:S(2)}) async-start(), calls=%async_computation.19 | async-start | bytes 1048576 | tf_op jit(solution)/shard_map/psum | solution.py:46
  412.8 97.9 %copy-start.114 = (f32[1024]{0:T(1024)S(1)}, f32[1024]{0:T(1024)}, u32[]{:S(2)}) copy-start(f32[1024]{0:T(1024)} %get-tuple-element.546) | copy-start | bytes 12292
  448.0 62.6 %copy-start.7 = (bf16[256,1024]{1,0:T(8,128)(2,1)S(1)}, bf16[256,1024]{1,0:T(8,128)(2,1)}, u32[]{:S(2)}) copy-start(bf16[256,1024]{1,0:T(8,128)(2,1)} %all-reduce.15.cloned.1.call-done) | copy-start | bytes 1572868
  449.4 63.8 %copy-start.59 = (f32[256]{0:T(256)}, f32[256]{0:T(256)S(1)}, u32[]{:S(2)}) copy-start(f32[256]{0:T(256)S(1)} %broadcast_multiply_fusion.14) | copy-start | bytes 3076
  450.7 62.5 %copy-start.105 = (f32[256]{0:T(256)}, f32[256]{0:T(256)S(1)}, u32[]{:S(2)}) copy-start(f32[256]{0:T(256)S(1)} %multiply_reduce_fusion.4) | copy-start | bytes 3076
  450.8 62.5 %copy-start.95 = (f32[256]{0:T(256)}, f32[256]{0:T(256)S(1)}, u32[]{:S(2)}) copy-start(f32[256]{0:T(256)S(1)} %fusion.133) | copy-start | bytes 3076
  616.3 108.4 %copy-start.3 = (f32[256,1024]{1,0:T(8,128)}, f32[256,1024]{1,0:T(8,128)S(1)}, u32[]{:S(2)}) copy-start(f32[256,1024]{1,0:T(8,128)S(1)} %get-tuple-element.513) | copy-start | bytes 3145732
  618.2 10.4 all-to-all-start.4
  628.6 9.4 all-to-all-start.5
  638.1 9.4 all-to-all-start.6
  641.4 83.3 %all-reduce.19.cloned.1.call-start = ((), (), s32[]{:S(2)}) async-start(), calls=%async_computation.20 | async-start | bytes 1048576 | tf_op jit(solution)/shard_map/psum | solution.py:46
  672.3 52.4 %copy-start.72 = (f32[1024]{0:T(1024)S(1)}, f32[1024]{0:T(1024)}, u32[]{:S(2)}) copy-start(f32[1024]{0:T(1024)} %get-tuple-element.550) | copy-start | bytes 12292
  683.3 104.1 %all-gather.15.cloned.1.call-start = ((), (), s32[]{:S(2)}) async-start(), calls=%async_computation.29 | async-start | bytes 4325376 | tf_op jit(solution)/shard_map/all_gather | solution.py:196
  684.1 153.5 %all-reduce.21.cloned.1.call-start = ((), (), s32[]{:S(2)}) async-start(), calls=%async_computation.21 | async-start | bytes 1048576 | tf_op jit(solution)/shard_map/psum | solution.py:46
  684.5 102.9 %copy-start.70 = (f32[1024]{0:T(1024)S(1)}, f32[1024]{0:T(1024)}, u32[]{:S(2)}) copy-start(f32[1024]{0:T(1024)} %get-tuple-element.552) | copy-start | bytes 12292
  726.0 113.7 %copy-start.5 = (f32[256,1024]{1,0:T(8,128)}, f32[256,1024]{1,0:T(8,128)S(1)}, u32[]{:S(2)}) copy-start(f32[256,1024]{1,0:T(8,128)S(1)} %get-tuple-element.511) | copy-start | bytes 3145732
  726.0 113.6 %copy-start.63 = (f32[256]{0:T(256)}, f32[256]{0:T(256)S(1)}, u32[]{:S(2)}) copy-start(f32[256]{0:T(256)S(1)} %broadcast_multiply_fusion.12) | copy-start | bytes 3076
  726.3 113.4 %copy-start.75 = (f32[256]{0:T(256)}, f32[256]{0:T(256)S(1)}, u32[]{:S(2)}) copy-start(f32[256]{0:T(256)S(1)} %fusion.135) | copy-start | bytes 3076
  845.8 10.4 all-to-all-start.8
  892.6 9.4 all-to-all-start.11
  902.1 9.4 all-to-all-start.10
  911.5 10.3 all-to-all-start.9
  915.7 49.0 %all-reduce.23.cloned.1.call-start = ((), (), s32[]{:S(2)}) async-start(), calls=%async_computation.22 | async-start | bytes 1048576 | tf_op jit(solution)/shard_map/psum | solution.py:46
  923.3 95.4 %all-reduce.25.cloned.1.call-start = ((), (), s32[]{:S(2)}) async-start(), calls=%async_computation.23 | async-start | bytes 1048576 | tf_op jit(solution)/shard_map/psum | solution.py:46
  970.4 53.5 %copy-start.10 = (f32[256,1024]{1,0:T(8,128)}, f32[256,1024]{1,0:T(8,128)S(1)}, u32[]{:S(2)}) copy-start(f32[256,1024]{1,0:T(8,128)S(1)} %get-tuple-element.497) | copy-start | bytes 3145732
  1027.3 10.4 all-to-all-start.12
  1072.9 9.6 all-to-all-start.15
  1082.6 9.4 all-to-all-start.14
  1092.0 9.4 all-to-all-start.13
  1095.3 51.9 %all-reduce.31.cloned.1.call-start = ((), (), s32[]{:S(2)}) async-start(), calls=%async_computation.32 | async-start | bytes 2097152 | tf_op jit(solution)/shard_map/psum | solution.py:46
  1102.9 197.3 %all-reduce.27.cloned.1.call-start = ((), (), s32[]{:S(2)}) async-start(), calls=%async_computation.30 | async-start | bytes 2097152
  1151.8 262.6 %all-reduce.29.cloned.1.call-start = ((), (), s32[]{:S(2)}) async-start(), calls=%async_computation.31 | async-start | bytes 8388608
  1156.1 400.6 %reduce-scatter.5.cloned.1.call-start = ((), (), s32[]{:S(2)}) async-start(), calls=%async_computation.25 | async-start | bytes 4325376 | tf_op jit(solution)/shard_map/reduce_scatter | solution.py:349
  1161.9 535.8 %reduce-scatter.3.cloned.1.call-start = ((), (), s32[]{:S(2)}) async-start(), calls=%async_computation.24 | async-start | bytes 4325376 | tf_op jit(solution)/shard_map/reduce_scatter | solution.py:349
  1170.2 130.7 %copy-start.62 = (f32[2,12,8]{1,2,0:T(8,128)S(1)}, f32[2,12,8]{1,2,0:T(8,128)}, u32[]{:S(2)}) copy-start(f32[2,12,8]{1,2,0:T(8,128)} %param.29) | copy-start | bytes 2308
  1170.2 130.7 %copy-start.112 = (f32[2,12,8]{1,2,0:T(8,128)S(1)}, f32[2,12,8]{1,2,0:T(8,128)}, u32[]{:S(2)}) copy-start(f32[2,12,8]{1,2,0:T(8,128)} %param.31) | copy-start | bytes 2308
  1170.2 130.7 %copy-start.113 = (f32[2,12,8]{1,2,0:T(8,128)S(1)}, f32[2,12,8]{1,2,0:T(8,128)}, u32[]{:S(2)}) copy-start(f32[2,12,8]{1,2,0:T(8,128)} %param.30) | copy-start | bytes 2308
  1170.2 245.1 %copy-start.42 = (f32[2,32,4,256]{3,2,1,0:T(4,128)S(1)}, f32[2,32,4,256]{3,2,1,0:T(4,128)}, u32[]{:S(2)}) copy-start(f32[2,32,4,256]{3,2,1,0:T(4,128)} %param.23) | copy-start | bytes 786436
  1173.8 524.0 %copy-start.25 = (f32[2,32,2,1024]{3,2,1,0:T(2,128)S(1)}, f32[2,32,2,1024]{3,2,1,0:T(2,128)}, u32[]{:S(2)}) copy-start(f32[2,32,2,1024]{3,2,1,0:T(2,128)} %param.26) | copy-start | bytes 1572868
  1173.8 524.0 %copy-start.51 = (f32[2,32,2,1024]{3,2,1,0:T(2,128)S(1)}, f32[2,32,2,1024]{3,2,1,0:T(2,128)}, u32[]{:S(2)}) copy-start(f32[2,32,2,1024]{3,2,1,0:T(2,128)} %param.28) | copy-start | bytes 1572868
  1173.8 524.0 %copy-start.52 = (f32[2,32,2,1024]{3,2,1,0:T(2,128)S(1)}, f32[2,32,2,1024]{3,2,1,0:T(2,128)}, u32[]{:S(2)}) copy-start(f32[2,32,2,1024]{3,2,1,0:T(2,128)} %param.27) | copy-start | bytes 1572868
  (116 other events, 966.8 us)
Sparse Core Ops, SparseCore 0:
  10.3 59.6 all-gather.8
  411.1 36.8 all-reduce.14
  450.3 60.2 all-gather.10
  512.8 56.5 all-gather.12
  572.1 42.5 all-reduce.16
  683.4 41.2 all-reduce.18
  727.0 60.2 all-gather.14
  794.9 42.6 all-reduce.20
  923.4 41.2 all-reduce.22
  975.0 43.6 all-reduce.24
  1103.0 44.2 all-reduce.30
  1152.7 147.4 all-reduce.26
  1303.5 110.7 all-reduce.28
  1416.6 140.0 reduce-scatter.4
  1558.9 138.8 reduce-scatter.2
where the time goes:
time: 1720 us; the launch traced here: 1710 us
  waiting for transfers between devices  1020 us (59%)
  blocking collectives  342 us (20%)
  local copies, waits for them, and re-layouts  93.2 us (5%)
  matrix products  86.7 us (5%)
  other arithmetic  81.1 us (5%)
  starting transfers between devices  52 us (3%)
    all_gather x1, blocking collectives, body(): lax.all_gather(vector_weight, ('fsdp', 'ctx', 'tp'), axis=2, tiled=True)  325 us
    reduce_scatter x2, waiting for transfers between devices, body(): lax.psum_scatter(feedforward_grads[layer_index].astype(jnp.bfloat16), ('f...  280 us
    psum x7, waiting for transfers between devices, tensor_sum(): lax.psum(partial_value.astype(jnp.bfloat16), 'tp').astype(jnp.float32)  263 us
    unnamed x17, waiting for transfers between devices  241 us
    all_gather x2, waiting for transfers between devices, body(): lax.all_gather(feedforward_weight[layer_index].astype(jnp.bfloat16), ('fs...  121 us
    all_gather x2, waiting for transfers between devices, body(): lax.all_gather(attention_weight[layer_index].astype(jnp.bfloat16), ('fsdp...  52 us
  transfers between devices with their start and end apart: 29, of which 28 were waited for; matrix products, arithmetic and copies ran while one was open for 5% of the time, Pallas kernels for 0%

commit v1 on v0

v1 whole, which is shorter than its diff:
```python
import jax
import jax.numpy as jnp
from jax import lax
from jax.experimental import pallas as pl
from jax.experimental.pallas import tpu as pltpu
from jax.sharding import PartitionSpec as P

H = 16
HD = 64
STEP = 10
FC = ("fsdp", "ctx")
NY = 4
NX = 4
TP = 4

norm_eps = 1e-05
gelu_factor = 0.7978845608028654
matrix_rate = 0.05
vector_rate = 0.3
weight_decay = 0.1

f32 = jnp.float32
bf16 = jnp.bfloat16
VMEM_LIMIT = 48 * 1024 * 1024


def place(y, x, core):
    return (y * 2 + (x & 1)) * 4 + (x >> 1) * 2 + core


def shift_perm(dy=0, dx=0, dc=0):
    return [
        (place(y, x, c), place((y + dy) % NY, (x + dx) % NX, (c + dc) % 2))
        for y in range(NY)
        for x in range(NX)
        for c in range(2)
    ]


def move(value, dy=0, dx=0, dc=0):
    return lax.ppermute(value, FC, shift_perm(dy, dx, dc))


def move_tp(value, k):
    return lax.ppermute(value, "tp", [(i, (i + k) % TP) for i in range(TP)])


def tp_gather(own):
    return jnp.concatenate([own] + [move_tp(own, k) for k in (1, 2, 3)], axis=0)


def tp_scatter(partial):
    rows = partial.shape[0] // TP
    total = partial[:rows].astype(f32)
    for k in (1, 2, 3):
        total = total + move_tp(partial[k * rows : (k + 1) * rows].astype(bf16), -k).astype(f32)
    return total


def turn_rows(values, t):
    rows = values.shape[0] // TP
    return jnp.concatenate(
        [lax.dynamic_slice_in_dim(values, ((t - k) & 3) * rows, rows, 0) for k in range(TP)], axis=0
    )


def tp_gather_natural(own, t):
    rows = own.shape[0]
    whole = jnp.zeros((rows * TP,) + own.shape[1:], own.dtype)
    whole = lax.dynamic_update_slice_in_dim(whole, own, t * rows, 0)
    for k in (1, 2, 3):
        whole = lax.dynamic_update_slice_in_dim(whole, move_tp(own, k), ((t - k) & 3) * rows, 0)
    return whole


def stage_gather(value, index_of, senders):
    count = len(senders) + 1
    whole = jnp.zeros((count,) + value.shape, value.dtype)
    whole = lax.dynamic_update_slice_in_dim(whole, value[None], index_of, 0)
    for received, index in senders:
        whole = lax.dynamic_update_slice_in_dim(whole, received[None], index, 0)
    return whole


def x_slot(x):
    return (x & 1) * 2 + (x >> 1)


def gather_vectors(own, y, x, core, t):
    layers, rows, width = own.shape
    value = own.reshape(1, layers * rows * width)
    value = stage_gather(value, t, [(move_tp(value, k), (t - k) & 3) for k in (1, 2, 3)])
    value = stage_gather(value, core, [(move(value, dc=1), 1 - core)])
    value = stage_gather(
        value, x_slot(x), [(move(value, dx=k), x_slot((x - k) & 3)) for k in (1, 2, 3)]
    )
    value = stage_gather(value, y, [(move(value, dy=k), (y - k) & 3) for k in (1, 2, 3)])
    value = value.reshape(-1, layers, rows, width)
    return value.transpose(1, 2, 0, 3).reshape(layers, rows, -1)


def scatter_vectors(whole, y, x, core, t):
    layers, rows, _ = whole.shape
    value = whole.reshape(layers, rows, 128, 8).transpose(2, 0, 1, 3)
    value = value.reshape(NY, NX, 2, TP, layers * rows * 8)

    def pick(array, index):
        return lax.dynamic_index_in_dim(array, index, 0, keepdims=False)

    value = pick(value, y) + sum(move(pick(value, (y + k) & 3), dy=k) for k in (1, 2, 3))
    value = pick(value, x_slot(x)) + sum(
        move(pick(value, x_slot((x + k) & 3)), dx=k) for k in (1, 2, 3)
    )
    value = pick(value, core) + move(pick(value, 1 - core), dc=1)
    value = pick(value, t) + sum(move_tp(pick(value, (t + k) & 3), k) for k in (1, 2, 3))
    return value.reshape(layers, rows, 8)


def gather_rows(own):
    count = 32
    spread = jnp.broadcast_to(own[None], (count,) + own.shape).reshape(-1, own.shape[1])
    return lax.all_to_all(spread, FC, split_axis=0, concat_axis=0, tiled=True)


def sum_rows(partial):
    pieces = lax.all_to_all(partial, FC, split_axis=0, concat_axis=0, tiled=True)
    return jnp.sum(pieces.reshape(32, -1, partial.shape[1]), axis=0, dtype=f32)


def kv_gather(own):
    across = move(own, dx=2)
    beside = move(own, dc=1)
    return [own, beside, across, move(across, dc=1)]


def kv_scatter(parts):
    own = parts[0].astype(f32) + move(parts[1], dc=1).astype(f32)
    far = (parts[2].astype(f32) + move(parts[3], dc=1).astype(f32)).astype(bf16)
    return own + move(far, dx=2).astype(f32)


def place_of(row, block, t):
    return block * 256 + (((t - (row >> 6)) & 3) << 6) + (row & 63)


def last_last(a, b):
    return lax.dot_general(a, b, (((1,), (1,)), ((), ())), preferred_element_type=f32)


def attend_kernel(meta, slopes, q_ref, kv0, kv1, kv2, kv3, out_ref):
    c, t, s1, s2 = meta[0], meta[1], meta[2], meta[3]
    blocks = (kv0, kv1, kv2, kv3)
    row_place = place_of(lax.broadcasted_iota(jnp.int32, (256, 1), 0), c, t)
    row_segment = (row_place >= s1).astype(jnp.int32) + (row_place >= s2).astype(jnp.int32)
    distances = []
    for k in range(4):
        key_place = place_of(lax.broadcasted_iota(jnp.int32, (1, 256), 1), c ^ k, t)
        key_segment = (key_place >= s1).astype(jnp.int32) + (key_place >= s2).astype(jnp.int32)
        gap = row_place - key_place
        allowed = (gap >= 0) & (row_segment == key_segment)
        distances.append(jnp.where(allowed, gap, -1).astype(f32))
    mixed = []
    for h in range(4):
        cols = slice(h * HD, (h + 1) * HD)
        value_cols = slice(256 + h * HD, 256 + (h + 1) * HD)
        query = q_ref[:, cols]
        slope = slopes[h]
        scores = [
            jnp.where(d >= 0, last_last(query, kv[:, cols]) * 0.125 - slope * d, -1e30)
            for d, kv in zip(distances, blocks)
        ]
        top = jnp.maximum(
            jnp.maximum(scores[0], scores[1]), jnp.maximum(scores[2], scores[3])
        ).max(axis=-1, keepdims=True)
        exponent = [jnp.exp(s - top) for s in scores]
        total = (exponent[0] + exponent[1] + exponent[2] + exponent[3]).sum(axis=-1, keepdims=True)
        scale = 1.0 / total
        mixed.append(
            sum(
                jnp.dot((e * scale).astype(bf16), kv[:, value_cols], preferred_element_type=f32)
                for e, kv in zip(exponent, blocks)
            )
        )
    out_ref[...] = jnp.concatenate(mixed, axis=1).astype(bf16)


def attend_back_kernel(
    meta, slopes, q_ref, do_ref, kv0, kv1, kv2, kv3, dq_ref, dkv0, dkv1, dkv2, dkv3
):
    c, t, s1, s2 = meta[0], meta[1], meta[2], meta[3]
    blocks = (kv0, kv1, kv2, kv3)
    back_blocks = (dkv0, dkv1, dkv2, dkv3)
    row_place = place_of(lax.broadcasted_iota(jnp.int32, (1, 256), 1), c, t)
    row_segment = (row_place >= s1).astype(jnp.int32) + (row_place >= s2).astype(jnp.int32)
    distances = []
    for k in range(4):
        key_place = place_of(lax.broadcasted_iota(jnp.int32, (256, 1), 0), c ^ k, t)
        key_segment = (key_place >= s1).astype(jnp.int32) + (key_place >= s2).astype(jnp.int32)
        gap = row_place - key_place
        allowed = (gap >= 0) & (row_segment == key_segment)
        distances.append(jnp.where(allowed, gap, -1).astype(f32))
    turned = [kv[:, :256].astype(f32).T.astype(bf16) for kv in blocks]
    back_query = []
    back_keys = [[] for _ in range(4)]
    back_values = [[] for _ in range(4)]
    for h in range(4):
        cols = slice(h * HD, (h + 1) * HD)
        value_cols = slice(256 + h * HD, 256 + (h + 1) * HD)
        query = q_ref[:, cols]
        back_rows = do_ref[:, cols]
        slope = slopes[h]
        scores = [
            jnp.where(d >= 0, last_last(kv[:, cols], query) * 0.125 - slope * d, -1e30)
            for d, kv in zip(distances, blocks)
        ]
        top = jnp.maximum(
            jnp.maximum(scores[0], scores[1]), jnp.maximum(scores[2], scores[3])
        ).max(axis=0, keepdims=True)
        exponent = [jnp.exp(s - top) for s in scores]
        total = (exponent[0] + exponent[1] + exponent[2] + exponent[3]).sum(axis=0, keepdims=True)
        scale = 1.0 / total
        probs = [e * scale for e in exponent]
        back_probs = [last_last(kv[:, value_cols], back_rows) for kv in blocks]
        products = [p * b for p, b in zip(probs, back_probs)]
        delta = (products[0] + products[1] + products[2] + products[3]).sum(axis=0, keepdims=True)
        turned_query = None
        for k in range(4):
            back_scores = (probs[k] * (back_probs[k] - delta)).astype(bf16)
            part = jnp.dot(turned[k][cols], back_scores, preferred_element_type=f32)
            turned_query = part if turned_query is None else turned_query + part
            back_keys[k].append(jnp.dot(back_scores, query, preferred_element_type=f32) * 0.125)
            back_values[k].append(
                jnp.dot(probs[k].astype(bf16), back_rows, preferred_element_type=f32)
            )
        back_query.append(turned_query)
    dq_ref[...] = (jnp.concatenate(back_query, axis=0) * 0.125).T.astype(bf16)
    for k in range(4):
        back_blocks[k][...] = jnp.concatenate(back_keys[k] + back_values[k], axis=1).astype(bf16)


SMEM = pl.BlockSpec(memory_space=pltpu.SMEM)
VMEM = pl.BlockSpec(memory_space=pltpu.VMEM)


def attend(meta, slopes, queries, kv_blocks):
    return pl.pallas_call(
        attend_kernel,
        out_shape=jax.ShapeDtypeStruct((256, 256), bf16),
        in_specs=[SMEM, SMEM] + [VMEM] * 5,
        out_specs=VMEM,
        compiler_params=pltpu.CompilerParams(vmem_limit_bytes=VMEM_LIMIT),
        name="attend",
    )(meta, slopes, queries, *kv_blocks)


def attend_back(meta, slopes, queries, back_mixed, kv_blocks):
    return pl.pallas_call(
        attend_back_kernel,
        out_shape=[jax.ShapeDtypeStruct((256, 256), bf16)]
        + [jax.ShapeDtypeStruct((256, 512), bf16)] * 4,
        in_specs=[SMEM, SMEM] + [VMEM] * 6,
        out_specs=[VMEM] * 5,
        compiler_params=pltpu.CompilerParams(vmem_limit_bytes=VMEM_LIMIT),
        name="attend_back",
    )(meta, slopes, queries, back_mixed, *kv_blocks)


def weight_grads(pairs):
    tokens = pairs[0][0].shape[0]
    height = pairs[0][0].shape[1]
    widths = [rhs.shape[1] for _, rhs in pairs]
    block = 256
    count = len(pairs)

    def kernel(*refs):
        out_ref = refs[-1]
        start = 0
        for i, width in enumerate(widths):
            out_ref[:, start : start + width] = lax.dot_general(
                refs[i][...],
                refs[count + i][...],
                (((0,), (0,)), ((), ())),
                preferred_element_type=f32,
            ).astype(bf16)
            start += width

    return pl.pallas_call(
        kernel,
        grid=(height // block,),
        out_shape=jax.ShapeDtypeStruct((height, sum(widths)), bf16),
        in_specs=[pl.BlockSpec((tokens, block), lambda i: (0, i))] * count
        + [pl.BlockSpec((tokens, w), lambda i: (0, 0)) for w in widths],
        out_specs=pl.BlockSpec((block, sum(widths)), lambda i: (i, 0)),
        compiler_params=pltpu.CompilerParams(vmem_limit_bytes=VMEM_LIMIT),
        name="weight_grads",
    )(*[lhs for lhs, _ in pairs], *[rhs for _, rhs in pairs])


def norm_parts(values):
    centre = values - jnp.mean(values, axis=-1, keepdims=True)
    spread = jnp.mean(centre * centre, axis=-1, keepdims=True)
    scale = lax.rsqrt(spread + norm_eps)
    return centre * scale, scale


def norm_back(back, unit, scale, gain_row):
    scaled = back * gain_row
    inner = scaled - jnp.mean(scaled, axis=-1, keepdims=True)
    inner = inner - unit * jnp.mean(scaled * unit, axis=-1, keepdims=True)
    return inner * scale, jnp.sum(back * unit, axis=0), jnp.sum(back, axis=0)


def gelu_tanh(values):
    return (
        0.5
        * values
        * (1.0 + jnp.tanh(gelu_factor * (values + 0.044715 * values * values * values)))
    )


def adamw_step(weight, moment, second, gradient, step_rate, decay_rate):
    moment = 0.9 * moment + 0.1 * gradient
    second = 0.95 * second + 0.05 * gradient * gradient
    first_fix = 1.0 - 0.9**STEP
    second_fix = 1.0 - 0.95**STEP
    update = moment / first_fix / (jnp.sqrt(second / second_fix) + 1e-08) + decay_rate * weight
    return (moment, second, weight - step_rate * update)


def matmul(a, b):
    return jnp.dot(a, b, preferred_element_type=f32)


def body(
    block_input,
    cotangent,
    sequence_starts,
    attention_weight,
    attention_first,
    attention_second,
    feedforward_weight,
    feedforward_first,
    feedforward_second,
    vector_weight,
    vector_first,
    vector_second,
):
    fsdp = lax.axis_index("fsdp")
    c = lax.axis_index("ctx")
    t = lax.axis_index("tp")
    y, x, core = fsdp >> 1, (fsdp & 1) + (c >> 1) * 2, c & 1
    rows = block_input.shape[0] // TP
    width = 256
    meta = jnp.stack([c, t, sequence_starts[0, 0], sequence_starts[0, 1]]).astype(jnp.int32)
    slopes = jnp.exp2(
        -8.0 * ((t * 4 + jnp.arange(4, dtype=jnp.int32)).astype(f32) + 1.0) / H
    )

    attention_low = attention_weight.astype(bf16)
    feedforward_low = feedforward_weight.astype(bf16)
    with jax.named_scope("gather_qkv0"):
        qkv0 = gather_rows(attention_low[0, :, :3].reshape(32, 3 * width))
    with jax.named_scope("gather_vectors"):
        vectors = gather_vectors(vector_weight, y, x, core, t)
    with jax.named_scope("gather_out0"):
        out0 = gather_rows(attention_low[0, :, 3])
    with jax.named_scope("gather_rest"):
        rest = lax.all_gather(
            jnp.stack(
                [
                    feedforward_low[0, :, 0],
                    feedforward_low[0, :, 1],
                    attention_low[1].reshape(32, 4 * width),
                    feedforward_low[1, :, 0],
                    feedforward_low[1, :, 1],
                ]
            ),
            FC,
            axis=1,
            tiled=True,
        )
    qkv_weight = (qkv0, rest[2][:, : 3 * width])
    out_weight = (out0, rest[2][:, 3 * width :])
    up_weight = (rest[0], rest[3])
    down_weight = (rest[1], rest[4])

    stream_full = turn_rows(block_input, t).astype(f32)
    stream = stream_full[:rows]
    kept = []
    for layer in range(2):
        vector = vectors[layer]
        bias_query = lax.dynamic_slice_in_dim(vector[2], t * width, width)
        bias_value = lax.dynamic_slice_in_dim(vector[3], t * width, width)
        bias_hidden = lax.dynamic_index_in_dim(vector[8:], t, 0, keepdims=False)
        with jax.named_scope(f"norm_one_{layer}"):
            if layer == 0:
                unit_full, scale_full = norm_parts(stream_full)
                unit_one, scale_one = unit_full[:rows], scale_full[:rows]
                normed = (unit_full * vector[0] + vector[1]).astype(bf16)
            else:
                unit_one, scale_one = norm_parts(stream)
                normed = tp_gather((unit_one * vector[0] + vector[1]).astype(bf16))
        with jax.named_scope(f"project_{layer}"):
            bias_kv = jnp.concatenate([jnp.zeros_like(bias_value), bias_value])
            kv_own = (matmul(normed, qkv_weight[layer][:, width:]) + bias_kv).astype(bf16)
            kv_blocks = kv_gather(kv_own)
            queries = (matmul(normed, qkv_weight[layer][:, :width]) + bias_query).astype(bf16)
        with jax.named_scope(f"attend_{layer}"):
            mixed = attend(meta, slopes, queries, kv_blocks)
        with jax.named_scope(f"out_{layer}"):
            middle = stream + tp_scatter(last_last(mixed, out_weight[layer])) + vector[4]
        with jax.named_scope(f"norm_two_{layer}"):
            unit_two, scale_two = norm_parts(middle)
            normed_two = tp_gather((unit_two * vector[5] + vector[6]).astype(bf16))
        with jax.named_scope(f"feedforward_{layer}"):
            hidden = matmul(normed_two, up_weight[layer]) + bias_hidden
            active = gelu_tanh(hidden).astype(bf16)
            stream = middle + tp_scatter(last_last(active, down_weight[layer])) + vector[7]
        kept.append(
            (
                normed,
                unit_one,
                scale_one,
                queries,
                kv_blocks,
                mixed,
                unit_two,
                scale_two,
                normed_two,
                hidden,
                active,
            )
        )
    with jax.named_scope("block_output"):
        block_output = tp_gather_natural(stream, t)

    back_branch = turn_rows(cotangent, t)
    back = back_branch[:rows].astype(f32)
    attention_grads = [None, None]
    feedforward_grads = [None, None]
    vector_grads = [None, None]
    for layer in (1, 0):
        (
            normed,
            unit_one,
            scale_one,
            queries,
            kv_blocks,
            mixed,
            unit_two,
            scale_two,
            normed_two,
            hidden,
            active,
        ) = kept[layer]
        vector = vectors[layer]
        with jax.named_scope(f"back_feedforward_{layer}"):
            if layer == 0:
                back_branch = tp_gather(back.astype(bf16))
            back_down_row = jnp.sum(back_branch[:rows].astype(f32), axis=0)
            back_active = matmul(back_branch, down_weight[layer])
            back_hidden = jax.vjp(gelu_tanh, hidden)[1](back_active)[0].astype(bf16)
            back_up_row = jnp.sum(back_hidden.astype(f32), axis=0)
            back_two = tp_scatter(last_last(back_hidden, up_weight[layer]))
        if layer == 1:
            with jax.named_scope(f"grads_feedforward_{layer}"):
                partial = weight_grads([(normed_two, back_hidden), (back_branch, active)])
                owned = lax.psum_scatter(partial, FC, scatter_dimension=0, tiled=True)
                feedforward_grads[layer] = owned.astype(f32).reshape(32, 2, 1024)
        with jax.named_scope(f"back_norm_two_{layer}"):
            step, back_gain_two, back_shift_two = norm_back(
                back_two, unit_two, scale_two, vector[5]
            )
            back_middle = back + step
            back_attn_own = back_middle.astype(bf16)
            back_attn = tp_gather(back_attn_own)
            back_out_row = jnp.sum(back_attn_own.astype(f32), axis=0)
        with jax.named_scope(f"back_attend_{layer}"):
            back_mixed = matmul(back_attn, out_weight[layer]).astype(bf16)
            back_query, *back_parts = attend_back(meta, slopes, queries, back_mixed, kv_blocks)
        if layer == 0:
            with jax.named_scope(f"grads_feedforward_{layer}"):
                owned_most = sum_rows(
                    weight_grads(
                        [(normed_two, back_hidden), (back_branch, active), (back_attn, mixed)]
                    )
                )
                feedforward_grads[layer] = owned_most[:, :2048].reshape(32, 2, 1024)
        with jax.named_scope(f"back_project_{layer}"):
            back_kv = kv_scatter(back_parts).astype(bf16)
            back_qkv = jnp.concatenate([back_query, back_kv], axis=1)
            back_one = tp_scatter(last_last(back_qkv, qkv_weight[layer]))
        with jax.named_scope(f"grads_attention_{layer}"):
            if layer == 1:
                owned = sum_rows(weight_grads([(normed, back_qkv), (back_attn, mixed)]))
            else:
                owned = jnp.concatenate(
                    [sum_rows(weight_grads([(normed, back_qkv)])), owned_most[:, 2048:]], axis=1
                )
            attention_grads[layer] = owned.reshape(32, 4, width)
        with jax.named_scope(f"back_norm_one_{layer}"):
            step, back_gain_one, back_shift_one = norm_back(
                back_one, unit_one, scale_one, vector[0]
            )
            back = back_middle + step
        with jax.named_scope(f"vector_grads_{layer}"):
            zero_row = jnp.zeros((1024,), f32)
            column_sums = jnp.sum(back_qkv.astype(f32), axis=0)
            query_row = lax.dynamic_update_slice_in_dim(
                zero_row, column_sums[:width], t * width, 0
            )
            value_row = lax.dynamic_update_slice_in_dim(
                zero_row, column_sums[2 * width :], t * width, 0
            )
            hidden_rows = lax.dynamic_update_slice_in_dim(
                jnp.zeros((4, 1024), f32), back_up_row[None], t, 0
            )
            vector_grads[layer] = jnp.concatenate(
                [
                    jnp.stack(
                        [
                            back_gain_one,
                            back_shift_one,
                            query_row,
                            value_row,
                            back_out_row,
                            back_gain_two,
                            back_shift_two,
                            back_down_row,
                        ]
                    ),
                    hidden_rows,
                ],
                axis=0,
            )
    with jax.named_scope("input_gradient"):
        input_gradient = tp_gather_natural(back, t)
    with jax.named_scope("scatter_vectors"):
        vector_total = scatter_vectors(jnp.stack(vector_grads), y, x, core, t)
    with jax.named_scope("adamw"):
        attention_out = adamw_step(
            attention_weight,
            attention_first,
            attention_second,
            jnp.stack(attention_grads),
            matrix_rate,
            weight_decay,
        )
        feedforward_out = adamw_step(
            feedforward_weight,
            feedforward_first,
            feedforward_second,
            jnp.stack(feedforward_grads),
            matrix_rate,
            weight_decay,
        )
        vector_out = adamw_step(
            vector_weight, vector_first, vector_second, vector_total, vector_rate, 0.0
        )
    return (block_output, input_gradient, *attention_out, *feedforward_out, *vector_out)


def solution(mesh):
    tokens = P(FC, None)
    weights = P(None, FC, None, "tp")
    vectors = P(None, None, ("fsdp", "ctx", "tp"))
    in_specs = (tokens, tokens, P("fsdp", None)) + (weights,) * 6 + (vectors,) * 3
    out_specs = (tokens,) * 2 + (weights,) * 6 + (vectors,) * 3
    return jax.shard_map(body, mesh=mesh, in_specs=in_specs, out_specs=out_specs, check_vma=False)
```

time: 1720 us -> 518 us (0.30)
  waiting for transfers between devices: 1020 us -> 173 us
  blocking collectives: 342 us -> 0 us
  starting transfers between devices: 52 us -> 145 us
  matrix products: 86.7 us -> 39.5 us
  local copies, waits for them, and re-layouts: 93.2 us -> 54.9 us
  other arithmetic: 81.1 us -> 47.1 us
  Pallas kernels: 0 us -> 32.1 us
    all_gather x1 -> x0, blocking collectives: 325 us -> none  [body(): lax.all_gather(vector_weight, ('fsdp', 'ctx', 'tp'), axis=2, tiled=True)]
    reduce_scatter x2 -> x1, waiting for transfers between devices: 280 us -> 0.01 us  [body(): owned = lax.psum_scatter(partial, FC, scatter_dimension=0, tiled=True)]
    psum x7 -> x0, waiting for transfers between devices: 263 us -> none  [tensor_sum(): lax.psum(partial_value.astype(jnp.bfloat16), 'tp').astype(jnp.float32)]
    unnamed x17 -> x2, waiting for transfers between devices: 241 us -> 0.03 us
    all_gather x4 -> x1, waiting for transfers between devices: 173 us -> 0.01 us  [body(): lax.all_gather(jnp.stack([feedforward_low[0, :, 0], feedforward_low[0, :,...]
    ppermute x0 -> x80, waiting for transfers between devices: none -> 162 us  [the longest x26 104 us: move(): return lax.ppermute(value, FC, shift_perm(dy, dx, dc))]
    ppermute x0 -> x80, starting transfers between devices: none -> 109 us  [the longest x54 77.3 us: move_tp(): return lax.ppermute(value, 'tp', [(i, (i + k) % TP) for i in range(TP)])]
    all_to_all x14 -> x5, waiting for transfers between devices: 66.2 us -> 10.4 us  [the longest x3 9.23 us: sum_rows(): lax.all_to_all(partial, FC, split_axis=0, concat_axis=0, tiled=True)]
  transfers between devices with their start and end apart: 29 -> 87, of which waited for: 28 -> 44; matrix products, arithmetic and copies ran while one was open for 5% -> 19% of each run, Pallas kernels for 0% -> 4%
where the time goes in v1:
time: 518 us; the launch traced here: 508 us
  waiting for transfers between devices  173 us (33%)
  starting transfers between devices  145 us (28%)
  local copies, waits for them, and re-layouts  54.9 us (11%)
  other arithmetic  47.1 us (9%)
  matrix products  39.5 us (8%)
  Pallas kernels  32.1 us (6%)
  between operations  16.7 us (3%)
    ppermute x26, waiting for transfers between devices, move(): return lax.ppermute(value, FC, shift_perm(dy, dx, dc))  104 us
    ppermute x54, starting transfers between devices, move_tp(): return lax.ppermute(value, 'tp', [(i, (i + k) % TP) for i in range(TP)])  77.3 us
    ppermute x54, waiting for transfers between devices, move_tp(): return lax.ppermute(value, 'tp', [(i, (i + k) % TP) for i in range(TP)])  58.5 us
    ppermute x26, starting transfers between devices, move(): return lax.ppermute(value, FC, shift_perm(dy, dx, dc))  31.7 us
    all_to_all x3, starting transfers between devices, sum_rows(): lax.all_to_all(partial, FC, split_axis=0, concat_axis=0, tiled=True)  22.2 us
    dot_general x10, matrix products, matmul(): return jnp.dot(a, b, preferred_element_type=f32)  20.4 us
    dot_general x8, matrix products, last_last(): lax.dot_general(a, b, (((1,), (1,)), ((), ())), preferred_element_type=f32)  19.1 us
    all_to_all x2, starting transfers between devices, gather_rows(): return lax.all_to_all(spread, FC, split_axis=0, concat_axis=0, tiled=True)  14 us
  transfers between devices with their start and end apart: 87, of which 44 were waited for; matrix products, arithmetic and copies ran while one was open for 19% of the time, Pallas kernels for 4%

profile of v1, /device:TPU:0, one launch (start us, length us, event | category | flops | bytes accessed | tf_op | source)
XLA Modules:
  0.0 508.0 jit_solution(5060264710723581353)
XLA Ops:
  12.5 3.6 collective-permute-start.1
  18.5 7.4 %all-to-all-start = ((bf16[32,32,768]{2,1,0:T(8,128)(2,1)}), bf16[32,32,768]{2,1,0:T(8,128)(2,1)}, u32[]{:S(2)}, u32[]{:S(2)}) async-start(bf16[32,32,768]{2,1,0:T(8,128)(2,1)} %broadcast_in_dim.111), calls=%async_computation | async-start | bytes 3145728 | tf_op jit(solution)/shard_map/gather_qkv0/all_to_all | solution.py:122
  29.8 2.7 collective-permute-start.5
  34.0 18.4 %collective-permute-done.4 = f32[2,4,1,192]{3,1,0,2:T(4,128)S(1)} collective-permute-done((f32[2,4,1,192]{3,1,0,2:T(4,128)S(1)}, f32[2,4,1,192]{3,1,0,2:T(4,128)S(1)}, u32[]{:S(2)}, u32[]{:S(2)}) %collective-permute-start.4) | collective-permute-done | bytes 6176 | tf_op jit(solution)/shard_map/gather_vectors/ppermute | solution.py:41
  52.4 6.7 %collective-permute-done.5 = f32[2,4,1,192]{3,1,0,2:T(4,128)S(1)} collective-permute-done((f32[2,4,1,192]{3,1,0,2:T(4,128)S(1)}, f32[2,4,1,192]{3,1,0,2:T(4,128)S(1)}, u32[]{:S(2)}, u32[]{:S(2)}) %collective-permute-start.5) | collective-permute-done | bytes 6176 | tf_op jit(solution)/shard_map/gather_vectors/ppermute | solution.py:41
  60.5 2.7 collective-permute-start.8
  68.7 3.4 slice_reduce_fusion
  77.5 6.5 %all-to-all-start.1 = ((bf16[32,32,256]{2,1,0:T(8,128)(2,1)}), bf16[32,32,256]{2,1,0:T(8,128)(2,1)S(1)}, u32[]{:S(2)}, u32[]{:S(2)}) async-start(bf16[32,32,256]{2,1,0:T(8,128)(2,1)} %broadcast_in_dim.113), calls=%async_computation.1 | async-start | bytes 1048576 | tf_op jit(solution)/shard_map/gather_out0/all_to_all | solution.py:122
  84.9 7.5 %collective-permute-done.11.kv2 = bf16[256,512]{1,0:T(8,128)(2,1)S(1)} collective-permute-done((bf16[256,512]{1,0:T(8,128)(2,1)S(1)}, bf16[256,512]{1,0:T(8,128)(2,1)S(1)}, u32[]{:S(2)}, u32[]{:S(2)}) %collective-permute-start.11) | collective-permute-done | bytes 262176 | tf_op jit(solution)/shard_map/project_0/ppermute | solution.py:41
  95.5 3.7 attend.2.refs_5_
  102.9 3.1 collective-permute-start.14
  121.8 3.3 collective-permute-done.16
  125.7 3.6 multiply_convert_fusion.1
  129.4 3.5 fusion.103
  132.9 2.7 collective-permute-start.19
  137.1 3.8 collective-permute-done.19
  151.7 3.3 collective-permute-done.22
  159.2 5.6 %collective-permute-done.26.kv2 = bf16[256,512]{1,0:T(8,128)(2,1)S(1)} collective-permute-done((bf16[256,512]{1,0:T(8,128)(2,1)S(1)}, bf16[256,512]{1,0:T(8,128)(2,1)S(1)}, u32[]{:S(2)}, u32[]{:S(2)}) %collective-permute-start.26) | collective-permute-done | bytes 262176 | tf_op jit(solution)/shard_map/project_1/ppermute | solution.py:41
  166.7 3.7 attend.3.refs_3_
  173.5 3.6 collective-permute-start.28
  180.8 2.9 collective-permute-done.28
  195.5 3.3 collective-permute-done.31
  199.5 2.8 multiply_convert_fusion
  202.3 3.8 convert_reduce_fusion.3
  232.0 4.1 collective-permute-done.43
  238.8 5.6 %attend_back.2 = (bf16[256,256]{1,0:T(8,128)(2,1)S(1)}, bf16[256,512]{1,0:T(8,128)(2,1)S(1)}, bf16[256,512]{1,0:T(8,128)(2,1)S(1)}, bf16[256,512]{1,0:T(8,128)(2,1)S(1)}, bf16[256,512]{1,0:T(8,128)(2,1)S(1)}) custom-call(s32[4]{0:T(128)S(1)} %pad_add_fusion.meta, f32[4]{0:T(128)S(1)} %multiply_exponential_fusion.slopes, bf16[256,256]{1,0:T(8,128)(2,1)S(1)} %copy-done.13, ...), custom_call_target="tpu_custom_call" | custom-call | tf_op jit(solution)/shard_map/back_attend_1/attend_back/pallas_call | solution.py:257
  253.2 3.8 collective-permute-done.48
  272.4 3.6 weight_grads.7
  276.0 2.7 collective-permute-start.37
  297.6 3.7 convert_reduce_fusion.4
  301.3 3.4 fusion.108
  305.4 2.7 collective-permute-start.55
  309.0 2.7 weight_grads.6
  311.8 6.5 %all-to-all-start.4 = ((bf16[32,32,1024]{2,1,0:T(8,128)(2,1)}), bf16[32,32,1024]{2,1,0:T(8,128)(2,1)}, u32[]{:S(2)}, u32[]{:S(2)}) async-start(bf16[32,32,1024]{2,1,0:T(8,128)(2,1)} %bitcast.42), calls=%async_computation.4 | async-start | bytes 4194304 | tf_op jit(solution)/shard_map/grads_attention_1/all_to_all | solution.py:126
  328.6 3.6 collective-permute-done.59
  333.8 6.3 %attend_back.3 = (bf16[256,256]{1,0:T(8,128)(2,1)S(1)}, bf16[256,512]{1,0:T(8,128)(2,1)S(1)}, bf16[256,512]{1,0:T(8,128)(2,1)S(1)}, bf16[256,512]{1,0:T(8,128)(2,1)S(1)}, bf16[256,512]{1,0:T(8,128)(2,1)}) custom-call(s32[4]{0:T(128)S(1)} %pad_add_fusion.meta, f32[4]{0:T(128)S(1)} %multiply_exponential_fusion.slopes, bf16[256,256]{1,0:T(8,128)(2,1)S(1)} %copy-done.11, ...), custom_call_target="tpu_custom_call" | custom-call | tf_op jit(solution)/shard_map/back_attend_0/attend_back/pallas_call | solution.py:257
  344.6 3.2 collective-permute-start.63
  348.5 6.3 %collective-permute-done.63 = bf16[256,512]{1,0:T(8,128)(2,1)S(1)} collective-permute-done((bf16[256,512]{1,0:T(8,128)(2,1)S(1)}, bf16[256,512]{1,0:T(8,128)(2,1)S(1)}, u32[]{:S(2)}, u32[]{:S(2)}) %collective-permute-start.63) | collective-permute-done | bytes 262176 | tf_op jit(solution)/shard_map/back_project_0/ppermute | solution.py:41
  357.6 8.1 %all-to-all-start.2 = ((bf16[32,32,768]{2,1,0:T(8,128)(2,1)}), bf16[32,32,768]{2,1,0:T(8,128)(2,1)}, u32[]{:S(2)}, u32[]{:S(2)}) async-start(bf16[32,32,768]{2,1,0:T(8,128)(2,1)} %bitcast.40), calls=%async_computation.2 | async-start | bytes 3145728 | tf_op jit(solution)/shard_map/grads_attention_0/all_to_all | solution.py:126
  371.9 3.9 weight_grads.5
  381.4 9.2 %all-to-all-done.2 = bf16[32,32,768]{2,1,0:T(8,128)(2,1)} async-done(((bf16[32,32,768]{2,1,0:T(8,128)(2,1)}), bf16[32,32,768]{2,1,0:T(8,128)(2,1)}, u32[]{:S(2)}, u32[]{:S(2)}) %all-to-all-start.2) | async-done | bytes 1572896 | tf_op jit(solution)/shard_map/grads_attention_0/all_to_all | solution.py:126
  390.6 7.5 %all-to-all-start.3 = ((bf16[32,32,2304]{2,1,0:T(8,128)(2,1)}), bf16[32,32,2304]{2,1,0:T(8,128)(2,1)}, u32[]{:S(2)}, u32[]{:S(2)}) async-start(bf16[32,32,2304]{2,1,0:T(8,128)(2,1)} %bitcast.169), calls=%async_computation.3 | async-start | bytes 9437184 | tf_op jit(solution)/shard_map/grads_feedforward_0/all_to_all | solution.py:126
  406.3 2.7 collective-permute-start.71
  412.1 46.9 %collective-permute-done.70 = f32[4,2,4,192]{3,2,1,0:T(4,128)S(1)} collective-permute-done((f32[4,2,4,192]{3,2,1,0:T(4,128)S(1)}, f32[4,2,4,192]{3,2,1,0:T(4,128)S(1)}, u32[]{:S(2)}, u32[]{:S(2)}) %collective-permute-start.70) | collective-permute-done | bytes 24608 | tf_op jit(solution)/shard_map/scatter_vectors/ppermute | solution.py:41
  459.3 3.1 collective-permute-start.75
  477.5 9.0 %collective-permute-done.67 = f32[64,1024]{1,0:T(8,128)S(1)} collective-permute-done((f32[64,1024]{1,0:T(8,128)S(1)}, f32[64,1024]{1,0:T(8,128)S(1)}, u32[]{:S(2)}, u32[]{:S(2)}) %collective-permute-start.67) | collective-permute-done | bytes 262176 | tf_op jit(solution)/shard_map/input_gradient/ppermute | solution.py:45
  491.2 3.0 convert_reduce_fusion
  497.9 2.8 multiply_subtract_fusion
  (630 shorter events, 225.1 us)
Async XLA Ops:
  7.2 118.5 %all-gather.2.cloned.1.call-start = ((), (), s32[]{:S(2)}) async-start(), calls=%async_computation.6 | async-start | bytes 10813440 | tf_op jit(solution)/shard_map/gather_rest/all_gather | solution.py:368
  10.5 16.2 %collective-permute-start = (f32[1,192]{1,0:T(1,128)S(1)}, f32[1,192]{1,0:T(1,128)S(1)}, u32[]{:S(2)}, u32[]{:S(2)}) collective-permute-start(f32[1,192]{1,0:T(1,128)S(1)} %reshape.256), channel_id=1, source_target_pairs={{0,1},{1,2},{2,3},{3,0},{4,5},{5,6},{6,7},{7,4},{8,9},{9,10},{10,1... | collective-permute-start | bytes 2312 | tf_op jit(solution)/shard_map/gather_vectors/ppermute | solution.py:45
  12.5 14.2 %collective-permute-start.1 = (f32[1,192]{1,0:T(1,128)S(1)}, f32[1,192]{1,0:T(1,128)S(1)}, u32[]{:S(2)}, u32[]{:S(2)}) collective-permute-start(f32[1,192]{1,0:T(1,128)S(1)} %reshape.256), channel_id=1, source_target_pairs={{0,2},{1,3},{2,0},{3,1},{4,6},{5,7},{6,4},{7,5},{8,10},{9,11},{10,... | collective-permute-start | bytes 2312 | tf_op jit(solution)/shard_map/gather_vectors/ppermute | solution.py:45
  16.1 10.7 %collective-permute-start.2 = (f32[1,192]{1,0:T(1,128)S(1)}, f32[1,192]{1,0:T(1,128)S(1)}, u32[]{:S(2)}, u32[]{:S(2)}) collective-permute-start(f32[1,192]{1,0:T(1,128)S(1)} %reshape.256), channel_id=1, source_target_pairs={{0,3},{1,0},{2,1},{3,2},{4,7},{5,4},{6,5},{7,6},{8,11},{9,8},{10,9... | collective-permute-start | bytes 2312 | tf_op jit(solution)/shard_map/gather_vectors/ppermute | solution.py:45
  18.5 55.8 %all-to-all-start = ((bf16[32,32,768]{2,1,0:T(8,128)(2,1)}), bf16[32,32,768]{2,1,0:T(8,128)(2,1)}, u32[]{:S(2)}, u32[]{:S(2)}) async-start(bf16[32,32,768]{2,1,0:T(8,128)(2,1)} %broadcast_in_dim.111), calls=%async_computation | async-start | bytes 3145728 | tf_op jit(solution)/shard_map/gather_qkv0/all_to_all | solution.py:122
  28.1 24.3 %collective-permute-start.4 = (f32[2,4,1,192]{3,1,0,2:T(4,128)S(1)}, f32[2,4,1,192]{3,1,0,2:T(4,128)S(1)}, u32[]{:S(2)}, u32[]{:S(2)}) collective-permute-start(f32[2,4,1,192]{3,1,0,2:T(4,128)S(1)} %constant_dynamic-update-slice_fusion.39), channel_id=1, source_target_pairs={{0,16},{4,20},{16,8},{20,12},{8,24},{12,28},{24,0},{28,4},{32,48},... | collective-permute-start | bytes 18440 | tf_op jit(solution)/shard_map/gather_vectors/ppermute | solution.py:41
  29.8 29.3 %collective-permute-start.5 = (f32[2,4,1,192]{3,1,0,2:T(4,128)S(1)}, f32[2,4,1,192]{3,1,0,2:T(4,128)S(1)}, u32[]{:S(2)}, u32[]{:S(2)}) collective-permute-start(f32[2,4,1,192]{3,1,0,2:T(4,128)S(1)} %constant_dynamic-update-slice_fusion.39), channel_id=1, source_target_pairs={{0,8},{4,12},{16,24},{20,28},{8,0},{12,4},{24,16},{28,20},{32,40},... | collective-permute-start | bytes 18440 | tf_op jit(solution)/shard_map/gather_vectors/ppermute | solution.py:41
  32.5 26.6 %collective-permute-start.6 = (f32[2,4,1,192]{3,1,0,2:T(4,128)S(1)}, f32[2,4,1,192]{3,1,0,2:T(4,128)S(1)}, u32[]{:S(2)}, u32[]{:S(2)}) collective-permute-start(f32[2,4,1,192]{3,1,0,2:T(4,128)S(1)} %constant_dynamic-update-slice_fusion.39), channel_id=1, source_target_pairs={{0,24},{4,28},{16,0},{20,4},{8,16},{12,20},{24,8},{28,12},{32,56},... | collective-permute-start | bytes 18440 | tf_op jit(solution)/shard_map/gather_vectors/ppermute | solution.py:41
  76.1 16.3 %collective-permute-start.11 = (bf16[256,512]{1,0:T(8,128)(2,1)S(1)}, bf16[256,512]{1,0:T(8,128)(2,1)S(1)}, u32[]{:S(2)}, u32[]{:S(2)}) collective-permute-start(bf16[256,512]{1,0:T(8,128)(2,1)S(1)} %fusion.12.kv0), channel_id=1, source_target_pairs={{0,8},{4,12},{16,24},{20,28},{8,0},{12,4},{24,16},{28,20},{32,40},... | collective-permute-start | bytes 786440 | tf_op jit(solution)/shard_map/project_0/ppermute | solution.py:41
  77.5 22.9 %all-to-all-start.1 = ((bf16[32,32,256]{2,1,0:T(8,128)(2,1)}), bf16[32,32,256]{2,1,0:T(8,128)(2,1)S(1)}, u32[]{:S(2)}, u32[]{:S(2)}) async-start(bf16[32,32,256]{2,1,0:T(8,128)(2,1)} %broadcast_in_dim.113), calls=%async_computation.1 | async-start | bytes 1048576 | tf_op jit(solution)/shard_map/gather_out0/all_to_all | solution.py:122
  84.0 412.6 %reduce-scatter.2.cloned.1.call-start = ((), (), s32[]{:S(2)}) async-start(), calls=%async_computation.7 | async-start | bytes 4325376 | tf_op jit(solution)/shard_map/grads_feedforward_1/reduce_scatter | solution.py:468
  84.7 10.8 %collective-permute-start.10 = (bf16[256,512]{1,0:T(8,128)(2,1)S(1)}, bf16[256,512]{1,0:T(8,128)(2,1)S(1)}, u32[]{:S(2)}, u32[]{:S(2)}) collective-permute-start(bf16[256,512]{1,0:T(8,128)(2,1)S(1)} %fusion.12.kv0), channel_id=1, source_target_pairs={{0,4},{4,0},{16,20},{20,16},{8,12},{12,8},{24,28},{28,24},{32,36},... | collective-permute-start | bytes 786440 | tf_op jit(solution)/shard_map/project_0/ppermute | solution.py:41
  115.9 9.2 %collective-permute-start.16 = (bf16[64,1024]{1,0:T(8,128)(2,1)S(1)}, bf16[64,1024]{1,0:T(8,128)(2,1)S(1)}, u32[]{:S(2)}, u32[]{:S(2)}) collective-permute-start(bf16[64,1024]{1,0:T(8,128)(2,1)S(1)} %add_convert_fusion.7), channel_id=1, source_target_pairs={{0,1},{1,2},{2,3},{3,0},{4,5},{5,6},{6,7},{7,4},{8,9},{9,10},{10,1... | collective-permute-start | bytes 393224 | tf_op jit(solution)/shard_map/norm_two_0/ppermute | solution.py:45
  146.1 8.9 %collective-permute-start.22 = (bf16[64,1024]{1,0:T(8,128)(2,1)S(1)}, bf16[64,1024]{1,0:T(8,128)(2,1)S(1)}, u32[]{:S(2)}, u32[]{:S(2)}) collective-permute-start(bf16[64,1024]{1,0:T(8,128)(2,1)S(1)} %add_convert_fusion.6), channel_id=1, source_target_pairs={{0,1},{1,2},{2,3},{3,0},{4,5},{5,6},{6,7},{7,4},{8,9},{9,10},{10,1... | collective-permute-start | bytes 393224 | tf_op jit(solution)/shard_map/norm_one_1/ppermute | solution.py:45
  146.2 8.8 %collective-permute-start.23 = (bf16[64,1024]{1,0:T(8,128)(2,1)S(1)}, bf16[64,1024]{1,0:T(8,128)(2,1)S(1)}, u32[]{:S(2)}, u32[]{:S(2)}) collective-permute-start(bf16[64,1024]{1,0:T(8,128)(2,1)S(1)} %add_convert_fusion.6), channel_id=1, source_target_pairs={{0,2},{1,3},{2,0},{3,1},{4,6},{5,7},{6,4},{7,5},{8,10},{9,11},{10,... | collective-permute-start | bytes 393224 | tf_op jit(solution)/shard_map/norm_one_1/ppermute | solution.py:45
  173.5 10.2 %collective-permute-start.28 = (bf16[64,1024]{1,0:T(8,128)(2,1)}, bf16[64,1024]{1,0:T(8,128)(2,1)S(1)}, u32[]{:S(2)}, u32[]{:S(2)}) collective-permute-start(bf16[64,1024]{1,0:T(8,128)(2,1)} %get-tuple-element.152), channel_id=1, source_target_pairs={{0,3},{1,0},{2,1},{3,2},{4,7},{5,4},{6,5},{7,6},{8,11},{9,8},{10,9... | collective-permute-start | bytes 393224 | tf_op jit(solution)/shard_map/out_1/ppermute | solution.py:45
  177.1 10.0 %collective-permute-start.30 = (bf16[64,1024]{1,0:T(8,128)(2,1)}, bf16[64,1024]{1,0:T(8,128)(2,1)}, u32[]{:S(2)}, u32[]{:S(2)}) collective-permute-start(bf16[64,1024]{1,0:T(8,128)(2,1)} %get-tuple-element.153), channel_id=1, source_target_pairs={{0,1},{1,2},{2,3},{3,0},{4,5},{5,6},{6,7},{7,4},{8,9},{9,10},{10,1... | collective-permute-start | bytes 393224 | tf_op jit(solution)/shard_map/out_1/ppermute | solution.py:45
  189.5 9.4 %collective-permute-start.31 = (bf16[64,1024]{1,0:T(8,128)(2,1)S(1)}, bf16[64,1024]{1,0:T(8,128)(2,1)}, u32[]{:S(2)}, u32[]{:S(2)}) collective-permute-start(bf16[64,1024]{1,0:T(8,128)(2,1)S(1)} %add_convert_fusion.5), channel_id=1, source_target_pairs={{0,1},{1,2},{2,3},{3,0},{4,5},{5,6},{6,7},{7,4},{8,9},{9,10},{10,1... | collective-permute-start | bytes 393224 | tf_op jit(solution)/shard_map/norm_two_1/ppermute | solution.py:45
  189.6 9.3 %collective-permute-start.32 = (bf16[64,1024]{1,0:T(8,128)(2,1)S(1)}, bf16[64,1024]{1,0:T(8,128)(2,1)}, u32[]{:S(2)}, u32[]{:S(2)}) collective-permute-start(bf16[64,1024]{1,0:T(8,128)(2,1)S(1)} %add_convert_fusion.5), channel_id=1, source_target_pairs={{0,2},{1,3},{2,0},{3,1},{4,6},{5,7},{6,4},{7,5},{8,10},{9,11},{10,... | collective-permute-start | bytes 393224 | tf_op jit(solution)/shard_map/norm_two_1/ppermute | solution.py:45
  208.7 10.5 %collective-permute-start.40 = (bf16[64,1024]{1,0:T(8,128)(2,1)S(1)}, bf16[64,1024]{1,0:T(8,128)(2,1)S(1)}, u32[]{:S(2)}, u32[]{:S(2)}) collective-permute-start(bf16[64,1024]{1,0:T(8,128)(2,1)S(1)} %get-tuple-element.143), channel_id=1, source_target_pairs={{0,3},{1,0},{2,1},{3,2},{4,7},{5,4},{6,5},{7,6},{8,11},{9,8},{10,9... | collective-permute-start | bytes 393224 | tf_op jit(solution)/shard_map/back_feedforward_1/ppermute | solution.py:45
  211.2 8.5 %collective-permute-start.41 = (bf16[64,1024]{1,0:T(8,128)(2,1)S(1)}, bf16[64,1024]{1,0:T(8,128)(2,1)S(1)}, u32[]{:S(2)}, u32[]{:S(2)}) collective-permute-start(bf16[64,1024]{1,0:T(8,128)(2,1)S(1)} %get-tuple-element.145), channel_id=1, source_target_pairs={{0,2},{1,3},{2,0},{3,1},{4,6},{5,7},{6,4},{7,5},{8,10},{9,11},{10,... | collective-permute-start | bytes 393224 | tf_op jit(solution)/shard_map/back_feedforward_1/ppermute | solution.py:45
  211.2 9.0 %collective-permute-start.42 = (bf16[64,1024]{1,0:T(8,128)(2,1)S(1)}, bf16[64,1024]{1,0:T(8,128)(2,1)S(1)}, u32[]{:S(2)}, u32[]{:S(2)}) collective-permute-start(bf16[64,1024]{1,0:T(8,128)(2,1)S(1)} %get-tuple-element.144), channel_id=1, source_target_pairs={{0,1},{1,2},{2,3},{3,0},{4,5},{5,6},{6,7},{7,4},{8,9},{9,10},{10,1... | collective-permute-start | bytes 393224 | tf_op jit(solution)/shard_map/back_feedforward_1/ppermute | solution.py:45
  227.8 8.3 %collective-permute-start.43 = (bf16[64,1024]{1,0:T(8,128)(2,1)S(1)}, bf16[64,1024]{1,0:T(8,128)(2,1)S(1)}, u32[]{:S(2)}, u32[]{:S(2)}) collective-permute-start(bf16[64,1024]{1,0:T(8,128)(2,1)S(1)} %get-tuple-element.108), channel_id=1, source_target_pairs={{0,1},{1,2},{2,3},{3,0},{4,5},{5,6},{6,7},{7,4},{8,9},{9,10},{10,1... | collective-permute-start | bytes 393224 | tf_op jit(solution)/shard_map/back_norm_two_1/ppermute | solution.py:45
  244.5 8.6 %collective-permute-start.46 = (bf16[256,512]{1,0:T(8,128)(2,1)S(1)}, bf16[256,512]{1,0:T(8,128)(2,1)}, u32[]{:S(2)}, u32[]{:S(2)}) collective-permute-start(bf16[256,512]{1,0:T(8,128)(2,1)S(1)} %get-tuple-element.23), channel_id=1, source_target_pairs={{0,4},{4,0},{16,20},{20,16},{8,12},{12,8},{24,28},{28,24},{32,36},... | collective-permute-start | bytes 786440 | tf_op jit(solution)/shard_map/back_project_1/ppermute | solution.py:41
  246.9 10.2 %collective-permute-start.48 = (bf16[256,512]{1,0:T(8,128)(2,1)}, bf16[256,512]{1,0:T(8,128)(2,1)}, u32[]{:S(2)}, u32[]{:S(2)}) collective-permute-start(bf16[256,512]{1,0:T(8,128)(2,1)} %add_convert_fusion.4), channel_id=1, source_target_pairs={{0,8},{4,12},{16,24},{20,28},{8,0},{12,4},{24,16},{28,20},{32,40},... | collective-permute-start | bytes 786440 | tf_op jit(solution)/shard_map/back_project_1/ppermute | solution.py:41
  260.6 23.3 %collective-permute-start.49 = (bf16[64,1024]{1,0:T(8,128)(2,1)}, bf16[64,1024]{1,0:T(8,128)(2,1)}, u32[]{:S(2)}, u32[]{:S(2)}) collective-permute-start(bf16[64,1024]{1,0:T(8,128)(2,1)} %get-tuple-element.140), channel_id=1, source_target_pairs={{0,3},{1,0},{2,1},{3,2},{4,7},{5,4},{6,5},{7,6},{8,11},{9,8},{10,9... | collective-permute-start | bytes 393224 | tf_op jit(solution)/shard_map/back_project_1/ppermute | solution.py:45
  263.1 22.0 %collective-permute-start.50 = (bf16[64,1024]{1,0:T(8,128)(2,1)}, bf16[64,1024]{1,0:T(8,128)(2,1)}, u32[]{:S(2)}, u32[]{:S(2)}) collective-permute-start(bf16[64,1024]{1,0:T(8,128)(2,1)} %get-tuple-element.142), channel_id=1, source_target_pairs={{0,2},{1,3},{2,0},{3,1},{4,6},{5,7},{6,4},{7,5},{8,10},{9,11},{10,... | collective-permute-start | bytes 393224 | tf_op jit(solution)/shard_map/back_project_1/ppermute | solution.py:45
  263.8 21.3 %collective-permute-start.51 = (bf16[64,1024]{1,0:T(8,128)(2,1)}, bf16[64,1024]{1,0:T(8,128)(2,1)}, u32[]{:S(2)}, u32[]{:S(2)}) collective-permute-start(bf16[64,1024]{1,0:T(8,128)(2,1)} %get-tuple-element.141), channel_id=1, source_target_pairs={{0,1},{1,2},{2,3},{3,0},{4,5},{5,6},{6,7},{7,4},{8,9},{9,10},{10,1... | collective-permute-start | bytes 393224 | tf_op jit(solution)/shard_map/back_project_1/ppermute | solution.py:45
  276.0 16.0 %collective-permute-start.37 = (f32[64,1024]{1,0:T(8,128)}, f32[64,1024]{1,0:T(8,128)}, u32[]{:S(2)}, u32[]{:S(2)}) collective-permute-start(f32[64,1024]{1,0:T(8,128)} %get-tuple-element.166), channel_id=1, source_target_pairs={{0,1},{1,2},{2,3},{3,0},{4,5},{5,6},{6,7},{7,4},{8,9},{9,10},{10,1... | collective-permute-start | bytes 786440 | tf_op jit(solution)/shard_map/block_output/ppermute | solution.py:45
  278.7 16.0 %collective-permute-start.38 = (f32[64,1024]{1,0:T(8,128)}, f32[64,1024]{1,0:T(8,128)S(1)}, u32[]{:S(2)}, u32[]{:S(2)}) collective-permute-start(f32[64,1024]{1,0:T(8,128)} %get-tuple-element.166), channel_id=1, source_target_pairs={{0,2},{1,3},{2,0},{3,1},{4,6},{5,7},{6,4},{7,5},{8,10},{9,11},{10,... | collective-permute-start | bytes 786440 | tf_op jit(solution)/shard_map/block_output/ppermute | solution.py:45
  283.9 126.5 %collective-permute-start.39 = (f32[64,1024]{1,0:T(8,128)}, f32[64,1024]{1,0:T(8,128)}, u32[]{:S(2)}, u32[]{:S(2)}) collective-permute-start(f32[64,1024]{1,0:T(8,128)} %get-tuple-element.166), channel_id=1, source_target_pairs={{0,3},{1,0},{2,1},{3,2},{4,7},{5,4},{6,5},{7,6},{8,11},{9,8},{10,9... | collective-permute-start | bytes 786440 | tf_op jit(solution)/shard_map/block_output/ppermute | solution.py:45
  305.4 12.9 %collective-permute-start.55 = (bf16[64,1024]{1,0:T(8,128)(2,1)}, bf16[64,1024]{1,0:T(8,128)(2,1)S(1)}, u32[]{:S(2)}, u32[]{:S(2)}) collective-permute-start(bf16[64,1024]{1,0:T(8,128)(2,1)} %get-tuple-element.137), channel_id=1, source_target_pairs={{0,3},{1,0},{2,1},{3,2},{4,7},{5,4},{6,5},{7,6},{8,11},{9,8},{10,9... | collective-permute-start | bytes 393224 | tf_op jit(solution)/shard_map/back_feedforward_0/ppermute | solution.py:45
  308.1 10.3 %collective-permute-start.56 = (bf16[64,1024]{1,0:T(8,128)(2,1)}, bf16[64,1024]{1,0:T(8,128)(2,1)S(1)}, u32[]{:S(2)}, u32[]{:S(2)}) collective-permute-start(bf16[64,1024]{1,0:T(8,128)(2,1)} %get-tuple-element.139), channel_id=1, source_target_pairs={{0,2},{1,3},{2,0},{3,1},{4,6},{5,7},{6,4},{7,5},{8,10},{9,11},{10,... | collective-permute-start | bytes 393224 | tf_op jit(solution)/shard_map/back_feedforward_0/ppermute | solution.py:45
  308.3 10.1 %collective-permute-start.57 = (bf16[64,1024]{1,0:T(8,128)(2,1)}, bf16[64,1024]{1,0:T(8,128)(2,1)}, u32[]{:S(2)}, u32[]{:S(2)}) collective-permute-start(bf16[64,1024]{1,0:T(8,128)(2,1)} %get-tuple-element.138), channel_id=1, source_target_pairs={{0,1},{1,2},{2,3},{3,0},{4,5},{5,6},{6,7},{7,4},{8,9},{9,10},{10,1... | collective-permute-start | bytes 393224 | tf_op jit(solution)/shard_map/back_feedforward_0/ppermute | solution.py:45
  311.8 45.8 %all-to-all-start.4 = ((bf16[32,32,1024]{2,1,0:T(8,128)(2,1)}), bf16[32,32,1024]{2,1,0:T(8,128)(2,1)}, u32[]{:S(2)}, u32[]{:S(2)}) async-start(bf16[32,32,1024]{2,1,0:T(8,128)(2,1)} %bitcast.42), calls=%async_computation.4 | async-start | bytes 4194304 | tf_op jit(solution)/shard_map/grads_attention_1/all_to_all | solution.py:126
  344.6 10.2 %collective-permute-start.63 = (bf16[256,512]{1,0:T(8,128)(2,1)S(1)}, bf16[256,512]{1,0:T(8,128)(2,1)S(1)}, u32[]{:S(2)}, u32[]{:S(2)}) collective-permute-start(bf16[256,512]{1,0:T(8,128)(2,1)S(1)} %add_convert_fusion.2), channel_id=1, source_target_pairs={{0,8},{4,12},{16,24},{20,28},{8,0},{12,4},{24,16},{28,20},{32,40},... | collective-permute-start | bytes 786440 | tf_op jit(solution)/shard_map/back_project_0/ppermute | solution.py:41
  357.6 33.1 %all-to-all-start.2 = ((bf16[32,32,768]{2,1,0:T(8,128)(2,1)}), bf16[32,32,768]{2,1,0:T(8,128)(2,1)}, u32[]{:S(2)}, u32[]{:S(2)}) async-start(bf16[32,32,768]{2,1,0:T(8,128)(2,1)} %bitcast.40), calls=%async_computation.2 | async-start | bytes 3145728 | tf_op jit(solution)/shard_map/grads_attention_0/all_to_all | solution.py:126
  377.8 22.0 %collective-permute-start.64 = (bf16[64,1024]{1,0:T(8,128)(2,1)S(1)}, bf16[64,1024]{1,0:T(8,128)(2,1)S(1)}, u32[]{:S(2)}, u32[]{:S(2)}) collective-permute-start(bf16[64,1024]{1,0:T(8,128)(2,1)S(1)} %get-tuple-element.134), channel_id=1, source_target_pairs={{0,3},{1,0},{2,1},{3,2},{4,7},{5,4},{6,5},{7,6},{8,11},{9,8},{10,9... | collective-permute-start | bytes 393224 | tf_op jit(solution)/shard_map/back_project_0/ppermute | solution.py:45
  379.7 20.1 %collective-permute-start.65 = (bf16[64,1024]{1,0:T(8,128)(2,1)S(1)}, bf16[64,1024]{1,0:T(8,128)(2,1)S(1)}, u32[]{:S(2)}, u32[]{:S(2)}) collective-permute-start(bf16[64,1024]{1,0:T(8,128)(2,1)S(1)} %get-tuple-element.136), channel_id=1, source_target_pairs={{0,2},{1,3},{2,0},{3,1},{4,6},{5,7},{6,4},{7,5},{8,10},{9,11},{10,... | collective-permute-start | bytes 393224 | tf_op jit(solution)/shard_map/back_project_0/ppermute | solution.py:45
  381.1 18.7 %collective-permute-start.66 = (bf16[64,1024]{1,0:T(8,128)(2,1)S(1)}, bf16[64,1024]{1,0:T(8,128)(2,1)S(1)}, u32[]{:S(2)}, u32[]{:S(2)}) collective-permute-start(bf16[64,1024]{1,0:T(8,128)(2,1)S(1)} %get-tuple-element.135), channel_id=1, source_target_pairs={{0,1},{1,2},{2,3},{3,0},{4,5},{5,6},{6,7},{7,4},{8,9},{9,10},{10,1... | collective-permute-start | bytes 393224 | tf_op jit(solution)/shard_map/back_project_0/ppermute | solution.py:45
  390.6 100.6 %all-to-all-start.3 = ((bf16[32,32,2304]{2,1,0:T(8,128)(2,1)}), bf16[32,32,2304]{2,1,0:T(8,128)(2,1)}, u32[]{:S(2)}, u32[]{:S(2)}) async-start(bf16[32,32,2304]{2,1,0:T(8,128)(2,1)} %bitcast.169), calls=%async_computation.3 | async-start | bytes 9437184 | tf_op jit(solution)/shard_map/grads_feedforward_0/all_to_all | solution.py:126
  404.3 54.7 %collective-permute-start.70 = (f32[4,2,4,192]{3,2,1,0:T(4,128)S(1)}, f32[4,2,4,192]{3,2,1,0:T(4,128)S(1)}, u32[]{:S(2)}, u32[]{:S(2)}) collective-permute-start(f32[4,2,4,192]{3,2,1,0:T(4,128)S(1)} %get-tuple-element.169), channel_id=1, source_target_pairs={{0,32},{4,36},{16,48},{20,52},{8,40},{12,44},{24,56},{28,60},{32,6... | collective-permute-start | bytes 73736 | tf_op jit(solution)/shard_map/scatter_vectors/ppermute | solution.py:41
  406.3 52.8 %collective-permute-start.71 = (f32[4,2,4,192]{3,2,1,0:T(4,128)S(1)}, f32[4,2,4,192]{3,2,1,0:T(4,128)S(1)}, u32[]{:S(2)}, u32[]{:S(2)}) collective-permute-start(f32[4,2,4,192]{3,2,1,0:T(4,128)S(1)} %get-tuple-element.167), channel_id=1, source_target_pairs={{0,64},{4,68},{16,80},{20,84},{8,72},{12,76},{24,88},{28,92},{32,9... | collective-permute-start | bytes 73736 | tf_op jit(solution)/shard_map/scatter_vectors/ppermute | solution.py:41
  409.0 50.1 %collective-permute-start.72 = (f32[4,2,4,192]{3,2,1,0:T(4,128)S(1)}, f32[4,2,4,192]{3,2,1,0:T(4,128)S(1)}, u32[]{:S(2)}, u32[]{:S(2)}) collective-permute-start(f32[4,2,4,192]{3,2,1,0:T(4,128)S(1)} %get-tuple-element.168), channel_id=1, source_target_pairs={{0,96},{4,100},{16,112},{20,116},{8,104},{12,108},{24,120},{28,124... | collective-permute-start | bytes 73736 | tf_op jit(solution)/shard_map/scatter_vectors/ppermute | solution.py:41
  467.3 9.4 %collective-permute-start.78 = (f32[192]{0:T(256)S(1)}, f32[192]{0:T(256)S(1)}, u32[]{:S(2)}, u32[]{:S(2)}) collective-permute-start(f32[192]{0:T(256)S(1)} %bitcast.191), channel_id=1, source_target_pairs={{0,2},{1,3},{2,0},{3,1},{4,6},{5,7},{6,4},{7,5},{8,10},{9,11},{10,... | collective-permute-start | bytes 2312 | tf_op jit(solution)/shard_map/scatter_vectors/ppermute | solution.py:45
  472.1 14.4 %collective-permute-start.67 = (f32[64,1024]{1,0:T(8,128)S(1)}, f32[64,1024]{1,0:T(8,128)S(1)}, u32[]{:S(2)}, u32[]{:S(2)}) collective-permute-start(f32[64,1024]{1,0:T(8,128)S(1)} %get-tuple-element.117), channel_id=1, source_target_pairs={{0,1},{1,2},{2,3},{3,0},{4,5},{5,6},{6,7},{7,4},{8,9},{9,10},{10,1... | collective-permute-start | bytes 786440 | tf_op jit(solution)/shard_map/input_gradient/ppermute | solution.py:45
  473.0 13.5 %collective-permute-start.68 = (f32[64,1024]{1,0:T(8,128)S(1)}, f32[64,1024]{1,0:T(8,128)S(1)}, u32[]{:S(2)}, u32[]{:S(2)}) collective-permute-start(f32[64,1024]{1,0:T(8,128)S(1)} %get-tuple-element.117), channel_id=1, source_target_pairs={{0,2},{1,3},{2,0},{3,1},{4,6},{5,7},{6,4},{7,5},{8,10},{9,11},{10,... | collective-permute-start | bytes 786440 | tf_op jit(solution)/shard_map/input_gradient/ppermute | solution.py:45
  474.2 13.0 %collective-permute-start.69 = (f32[64,1024]{1,0:T(8,128)S(1)}, f32[64,1024]{1,0:T(8,128)S(1)}, u32[]{:S(2)}, u32[]{:S(2)}) collective-permute-start(f32[64,1024]{1,0:T(8,128)S(1)} %get-tuple-element.117), channel_id=1, source_target_pairs={{0,3},{1,0},{2,1},{3,2},{4,7},{5,4},{6,5},{7,6},{8,11},{9,8},{10,9... | collective-permute-start | bytes 786440 | tf_op jit(solution)/shard_map/input_gradient/ppermute | solution.py:45
  (155 other events, 1517.9 us)
Sparse Core Ops, SparseCore 0:
  10.4 99.7 all-gather.1
  276.1 183.7 reduce-scatter.1
